TPU v7x, 256 devices: a whole 4x4x8 slice. The times are simulated.
256 devices in a mesh: gx: 16 (over z_hi, x), gy: 4 (over y), gz: 4 (over z_lo, core).
Axes of the slice: x: 4, y: 4, z: 8 (z_hi: 4, z_lo: 2; z = z_hi * 2 + z_lo), core: 2. Of those that a mesh axis runs over, the one named last changes fastest.
Arguments:
- fluid_populations: float32 [19, 64, 64, 512], P(None, 'gx', 'gy', 'gz'), may hold values from 0 to 10, as said below
- order_populations: float32 [19, 64, 64, 512], P(None, 'gx', 'gy', 'gz'), may hold values from -0.5 to 0.5
- plane_offsets: int32 [2, 4], replicated, may hold values from 0 to 63
- plane_weights: float32 [4], replicated, may hold values from 0.1 to 0.9
Outputs:
- fluid_next: float32 [19, 64, 64, 512], P(None, 'gx', 'gy', 'gz')
- order_next: float32 [19, 64, 64, 512], P(None, 'gx', 'gy', 'gz')
Inputs may be any that keep to these rules, and one draw needn't show every extreme that they name: `fluid_populations`: every entry is positive.
All inputs are finite; a program needn't handle non-finite values.
Results may differ from a plain program's by a relative error of at most 0.0001.
Values sent between devices are 32-bit elements; how exact they have to be, the bound alone decides.
No kernel may reach another device: no remote copies, remote signals or barrier semaphores. Data moves between devices by JAX's collectives and lax.ppermute only.
A program may use at most 128 MiB of HBM per device.

v0:
```python
import functools

import jax
import jax.numpy as jnp
from jax import lax
from jax.experimental import pallas as pl
from jax.experimental.pallas import tpu as pltpu
from jax.sharding import PartitionSpec as P

STEPS = 2

VELOCITIES = [
    (0, 0, 0),
    (1, 0, 0),
    (-1, 0, 0),
    (0, 1, 0),
    (0, -1, 0),
    (0, 0, 1),
    (0, 0, -1),
    (1, 1, 0),
    (-1, -1, 0),
    (1, -1, 0),
    (-1, 1, 0),
    (1, 0, 1),
    (-1, 0, -1),
    (1, 0, -1),
    (-1, 0, 1),
    (0, 1, 1),
    (0, -1, -1),
    (0, 1, -1),
    (0, -1, 1),
]
WEIGHTS = [1.0 / 3.0] + [1.0 / 18.0] * 6 + [1.0 / 36.0] * 12
RISING = [3, 7, 10, 15, 17]
FALLING = [4, 8, 9, 16, 18]
EAST = [i for i, c in enumerate(VELOCITIES) if c[0] == 1]
WEST = [i for i, c in enumerate(VELOCITIES) if c[0] == -1]
FRONT = [i for i, c in enumerate(VELOCITIES) if c[2] == 1]
BACK = [i for i, c in enumerate(VELOCITIES) if c[2] == -1]
A = -0.0625
B = 0.0625
K = 0.04
M = 0.5
TAU_F = 0.8
TAU_G = 0.9
U = 0.05

OWN = 8
BELOW_EDGE = 2
ABOVE_EDGE = 28
ITEMS = 17

VMEM = pl.BlockSpec(memory_space=pltpu.VMEM)
SMEM = pl.BlockSpec(memory_space=pltpu.SMEM)
F32 = jnp.float32


def call(body, outs, operands, specs, scratch=(), name=None):
    return pl.pallas_call(
        body,
        out_shape=[jax.ShapeDtypeStruct(shape, F32) for shape in outs],
        in_specs=specs,
        out_specs=[VMEM] * len(outs),
        scratch_shapes=list(scratch),
        compiler_params=pltpu.CompilerParams(vmem_limit_bytes=32 * 1024 * 1024),
        name=name,
    )(*operands)


def lanes(shape):
    return lax.broadcasted_iota(jnp.int32, shape, 1)


def rows_of(shape):
    return lax.broadcasted_iota(jnp.int32, shape, 0)


def shift(value, amount, axis):
    amount = amount % value.shape[axis]
    return value if amount == 0 else pltpu.roll(value, amount, axis)


def plane_shift(offsets, step, plane):
    return lax.rem(offsets[step, plane] + 2, 4) - 2


def planes():
    block = lax.axis_index("gy")
    return block, lax.rem(block + 3, 4)


def is_odd(axis):
    return lax.rem(lax.axis_index(axis), 2) == 1


def swapped(odd, one, two):
    return jnp.where(odd, two, one), jnp.where(odd, one, two)


def edge_messages(fluid, order, phase_ref, keep_ref, give_ref):
    odd = is_odd("gz")

    def put(item, x, low, high):
        keep, give = swapped(odd, high, low)
        keep_ref[item, x : x + 1, :] = keep
        give_ref[item, x : x + 1, :] = give

    for x in range(4):
        f = [fluid(i, x) for i in range(19)]
        g = [order(i, x) for i in range(19)]
        phase = sum(g[1:], g[0])
        phase_ref[x] = phase
        for item in range(3):
            put(item, x, phase[item : item + 1], phase[13 + item : 14 + item])
        fields = [sum(f[1:], f[0])]
        for q in range(3):
            plus = [f[i] for i, c in enumerate(VELOCITIES) if c[q] == 1]
            minus = [f[i] for i, c in enumerate(VELOCITIES) if c[q] == -1]
            fields.append(sum(plus[1:], plus[0]) - sum(minus[1:], minus[0]))
        for n, field in enumerate(fields):
            put(3 + n, x, field[0:1], field[15:16])
        for n in range(5):
            put(7 + n, x, f[FALLING[n]][0:1], f[RISING[n]][15:16])
            put(12 + n, x, g[FALLING[n]][0:1], g[RISING[n]][15:16])


def first_kernel(f_ref, g_ref, *rest):
    edge_messages(lambda i, x: f_ref[i, x], lambda i, x: g_ref[i, x], *rest)


def pair_kernel(keep_ref, got_ref, pair_ref):
    pair_ref[0] = keep_ref[...]
    pair_ref[1] = got_ref[...]


def stack_kernel(phase_ref, crossed_ref, other_ref, stack_ref, edge_ref):
    odd = is_odd("gz")
    stack_ref[...] = jnp.zeros_like(stack_ref)
    for x in range(4):
        stack_ref[x, OWN : OWN + 16, :] = phase_ref[x]
    for item in range(ITEMS):
        above, below = swapped(odd, crossed_ref[1, item], other_ref[0, item])
        if item < 3:
            for x in range(4):
                stack_ref[x, item : item + 1, :] = below[x : x + 1]
                stack_ref[x, ABOVE_EDGE + item : ABOVE_EDGE + item + 1, :] = above[x : x + 1]
        else:
            edge_ref[item - 3, 0:4, :] = below
            edge_ref[item - 3, 4:8, :] = above


def ghost_kernel(
    step, offsets, weights, own_ref, one_ref, two_ref, phase_ref, send_one, send_two, wide
):
    up, down = planes()
    r_down = plane_shift(offsets, step, down)
    r_up = plane_shift(offsets, step, up)
    w_down = weights[down]
    w_up = weights[up]
    odd = is_odd("gx")
    wide[4:8] = own_ref[...]
    for x in range(4):
        east, west = swapped(odd, one_ref[x], two_ref[x])
        wide[x] = west
        wide[8 + x] = east
    shape = (32, 128)
    row = rows_of(shape)
    lane = lanes(shape)
    first = jnp.zeros(shape, F32)
    last = jnp.zeros(shape, F32)

    def rise(place, r, w):
        return w * wide[place - r] + (1.0 - w) * wide[place - r - 1]

    def fall(place, r, w):
        return w * wide[place + r] + (1.0 - w) * wide[place + r + 1]

    for n in range(8):
        place = n + 2
        value = wide[place]
        if 1 <= n <= 6:
            value = jnp.where((row == 6) | (row == 7), shift(rise(place, r_down, w_down), 5, 0), value)
            value = jnp.where((row == 3) | (row == 4), shift(fall(place, r_down, w_down), -5, 0), value)
            value = jnp.where((row == 24) | (row == 25), shift(fall(place, r_up, w_up), -4, 0), value)
            value = jnp.where((row == 26) | (row == 27), shift(rise(place, r_up, w_up), 4, 0), value)
        phase_ref[n] = value
        first = jnp.where(lane // 2 == n, shift(value, 2 * n, 1), first)
        last = jnp.where(lane // 2 == n, shift(value, 2 * n - 126, 1), last)
    send_one[...], send_two[...] = swapped(is_odd("gz"), last, first)


def bulk_potential(phase, around):
    return A * phase + B * phase * phase * phase - K * (around - 6.0 * phase)


def collide_kernel(
    phase_ref,
    sent_one,
    sent_two,
    got_one,
    got_two,
    edge_ref,
    f_ref,
    g_ref,
    post_ref,
    send_one,
    send_two,
    ghost,
    pots,
    east,
    west,
):
    shape = (32, 128)
    lane = lanes(shape)
    odd = is_odd("gz")
    last, first = swapped(odd, sent_one[...], sent_two[...])
    right, left = swapped(odd, got_one[...], got_two[...])

    def updown(value):
        return shift(value, 1, 0) + shift(value, -1, 0)

    left_pot = bulk_potential(
        left, shift(left, 2, 1) + shift(left, -2, 1) + updown(left) + shift(left, 1, 1) + shift(first, 1, 1)
    )
    right_pot = bulk_potential(
        right,
        shift(right, 2, 1) + shift(right, -2, 1) + updown(right) + shift(right, -1, 1) + shift(last, -1, 1),
    )
    for n in range(1, 7):
        value = phase_ref[n]
        before = jnp.where(lane == 0, shift(left, -(2 * n + 1), 1), shift(value, 1, 1))
        after = jnp.where(lane == 127, shift(right, 127 - 2 * n, 1), shift(value, -1, 1))
        around = phase_ref[n - 1] + phase_ref[n + 1] + updown(value) + before + after
        pots[n] = bulk_potential(value, around)

    for x in range(4):
        n = x + 2
        phase_all = phase_ref[n]
        pot_all = pots[n]
        gx_all = 0.5 * (pots[n + 1] - pots[n - 1])
        gy_all = 0.5 * (shift(pot_all, -1, 0) - shift(pot_all, 1, 0))
        before = jnp.where(lane == 0, shift(left_pot, -(2 * n + 1), 1), shift(pot_all, 1, 1))
        after = jnp.where(lane == 127, shift(right_pot, 127 - 2 * n, 1), shift(pot_all, -1, 1))
        gz_all = 0.5 * (after - before)
        for k, value in enumerate((phase_all, pot_all, gx_all, gy_all, gz_all)):
            ghost[k, x : x + 1, :] = value[BELOW_EDGE : BELOW_EDGE + 1]
            ghost[k, 4 + x : 5 + x, :] = value[ABOVE_EDGE : ABOVE_EDGE + 1]
        own = slice(OWN, OWN + 16)
        phase = phase_all[own]
        pot = pot_all[own]
        grad = (gx_all[own], gy_all[own], gz_all[own])

        f = [f_ref[i, x] for i in range(19)]
        density = sum(f[1:], f[0])
        momentum = []
        for q in range(3):
            plus = [f[i] for i, c in enumerate(VELOCITIES) if c[q] == 1]
            minus = [f[i] for i, c in enumerate(VELOCITIES) if c[q] == -1]
            momentum.append(sum(plus[1:], plus[0]) - sum(minus[1:], minus[0]))
        inverse = 1.0 / density
        speed = [m * inverse for m in momentum]
        force = TAU_F * phase * inverse
        shifted = [s - force * d for s, d in zip(speed, grad)]
        square = shifted[0] * shifted[0] + shifted[1] * shifted[1] + shifted[2] * shifted[2]
        rest = 1.0 - 1.5 * square
        keep_f = 1.0 - 1.0 / TAU_F
        keep_g = 1.0 - 1.0 / TAU_G

        def store(i, fs, gs):
            post_ref[i, x] = fs
            post_ref[19 + i, x] = gs
            if x == 3 and i in EAST:
                k = EAST.index(i)
                east[k] = fs
                east[5 + k] = gs
            if x == 0 and i in WEST:
                k = WEST.index(i)
                west[k] = fs
                west[5 + k] = gs

        store(
            0,
            keep_f * f[0] + (WEIGHTS[0] / TAU_F) * density * rest,
            keep_g * g_ref[0, x] + (1.0 / TAU_G) * (phase - 2.0 * M * pot),
        )
        flow_scale = 3.0 * phase
        for i in range(1, 19, 2):
            along = directed(VELOCITIES[i], shifted)
            flow = directed(VELOCITIES[i], speed)
            scale = (WEIGHTS[i] / TAU_F) * density
            even = scale * (rest + 4.5 * along * along)
            odd = scale * (3.0 * along)
            g_even = (WEIGHTS[i] / TAU_G * 3.0 * M) * pot
            g_odd = (WEIGHTS[i] / TAU_G) * (flow_scale * flow)
            store(i, keep_f * f[i] + (even + odd), keep_g * g_ref[i, x] + (g_even + g_odd))
            store(i + 1, keep_f * f[i + 1] + (even - odd), keep_g * g_ref[i + 1, x] + (g_even - g_odd))

    sign = jnp.where(rows_of((8, 128)) < 4, 1.0, -1.0)
    phase, pot, gx, gy, gz = (ghost[k] for k in range(5))
    density = edge_ref[0]
    inverse = 1.0 / density
    speed = [edge_ref[1 + q] * inverse for q in range(3)]
    force = TAU_F * phase * inverse
    shifted = [s - force * d for s, d in zip(speed, (gx, gy, gz))]
    square = shifted[0] * shifted[0] + shifted[1] * shifted[1] + shifted[2] * shifted[2]
    rest = 1.0 - 1.5 * square
    for k, i in enumerate(RISING):
        along = sign * directed(VELOCITIES[i], shifted)
        flow = sign * directed(VELOCITIES[i], speed)
        feq = WEIGHTS[i] * density * (rest + 3.0 * along + 4.5 * along * along)
        fs = (1.0 - 1.0 / TAU_F) * edge_ref[4 + k] + (1.0 / TAU_F) * feq
        fs = fs - (3.0 * WEIGHTS[i] * VELOCITIES[i][0] * U) * density
        geq = WEIGHTS[i] * (3.0 * M * pot + 3.0 * phase * flow)
        gs = (1.0 - 1.0 / TAU_G) * edge_ref[9 + k] + (1.0 / TAU_G) * geq
        for ref in (send_one, send_two):
            ref[k, 16:24, :] = fs
            ref[5 + k, 16:24, :] = gs
    odd = is_odd("gx")
    for k in range(10):
        send_one[k, 0:16, :], send_two[k, 0:16, :] = swapped(odd, east[k], west[k])


def directed(velocity, parts):
    total = None
    for c, part in zip(velocity, parts):
        if c == 1:
            total = part if total is None else total + part
        elif c == -1:
            total = -part if total is None else total - part
    return total


def stream_kernel(
    step, offsets, weights, post_ref, own_ref, one_ref, two_ref, out_ref, send_one, send_two, wide
):
    up, down = planes()
    r_down = plane_shift(offsets, step, down)
    r_up = plane_shift(offsets, step, up)
    w_down = weights[down]
    w_up = weights[up]
    odd = is_odd("gx")
    for k in range(10):
        from_east, from_west = swapped(odd, one_ref[k, 16:24, :], two_ref[k, 16:24, :])
        for place, rows in enumerate((from_west, own_ref[k, 16:24, :], from_east)):
            for side in (0, 1):
                for x in range(4):
                    at = 4 * side + x
                    wide[side, 4 * place + x, k : k + 1, :] = rows[at : at + 1]
    shape = (16, 128)
    row = rows_of(shape)
    lane = lanes(shape)
    first = jnp.zeros(shape, F32)
    last = jnp.zeros(shape, F32)
    for x in range(4):
        place = x + 4
        risen = {}
        fallen = {}
        for c in (-1, 0, 1):
            at = place - c - r_down
            risen[c] = w_down * wide[0, at] + (1.0 - w_down) * wide[0, at - 1]
            at = place - c + r_up
            fallen[c] = w_up * wide[1, at] + (1.0 - w_up) * wide[1, at + 1]
        for i in range(38):
            part, component = divmod(i, 19)
            cx, cy, cz = VELOCITIES[component]
            source = x - cx
            if source < 0:
                k = 5 * part + EAST.index(component)
                value = jnp.where(odd, one_ref[k, 0:16, :], two_ref[k, 0:16, :])
            elif source > 3:
                k = 5 * part + WEST.index(component)
                value = jnp.where(odd, two_ref[k, 0:16, :], one_ref[k, 0:16, :])
            else:
                value = post_ref[i, source]
            if cy == 1:
                k = 5 * part + RISING.index(component)
                value = jnp.where(row == 0, risen[cx][k : k + 1], shift(value, 1, 0))
            elif cy == -1:
                k = 5 * part + FALLING.index(component)
                value = jnp.where(row == 15, fallen[cx][k : k + 1], shift(value, -1, 0))
            out_ref[i, x] = value
            if cz == 1:
                at = 4 * (5 * part + FRONT.index(component)) + x
                last = jnp.where(lane == at, shift(value, at - 127, 1), last)
            elif cz == -1:
                at = 4 * (5 * part + BACK.index(component)) + x
                first = jnp.where(lane == at, shift(value, at, 1), first)
    send_one[...], send_two[...] = swapped(is_odd("gz"), last, first)


def finish_kernel(more, moved_ref, one_ref, two_ref, f_ref, g_ref, *rest):
    lane = lanes((16, 128))
    right, left = swapped(is_odd("gz"), one_ref[...], two_ref[...])
    for x in range(4):
        for i in range(38):
            part, component = divmod(i, 19)
            value = moved_ref[i, x]
            cz = VELOCITIES[component][2]
            if cz == 1:
                at = 4 * (5 * part + FRONT.index(component)) + x
                value = jnp.where(lane == 0, shift(left, -at, 1), shift(value, 1, 1))
            elif cz == -1:
                at = 4 * (5 * part + BACK.index(component)) + x
                value = jnp.where(lane == 127, shift(right, 127 - at, 1), shift(value, -1, 1))
            (g_ref if part else f_ref)[component, x] = value
    if more:
        edge_messages(lambda i, x: f_ref[i, x], lambda i, x: g_ref[i, x], *rest)


def swap(axis, values, parity):
    count = lax.axis_size(axis)
    pairs = []
    for low in range(parity, count, 2):
        high = (low + 1) % count
        pairs += [(low, high), (high, low)]
    return lax.ppermute(values, axis, pairs)


def plane_pairs(count_x, blocks_y, count_z, steps):
    def number(x, y, z):
        return (x % count_x * blocks_y + y % blocks_y) * count_z + z

    pairs = []
    for x in range(count_x):
        for y in range(blocks_y):
            for z in range(0, count_z, 2):
                pairs.append((number(x, y, z), number(x + steps, y + 1, z + 1)))
                pairs.append((number(x + steps, y + 1, z + 1), number(x, y, z)))
    return pairs


def cross_planes(rows, steps):
    axes = ("gx", "gy", "gz")
    sizes = [lax.axis_size(axis) for axis in axes]

    def branch(number):
        pairs = plane_pairs(*sizes, number)
        return lambda sent: lax.ppermute(sent, axes, pairs)

    return lax.switch(steps, [branch(number) for number in range(sizes[0])], rows)


def per_device(fluid, order, offsets, weights):
    plane = (lax.axis_index("gy") + 3 * (lax.axis_index("gz") % 2)) % 4
    steps = (offsets[:, plane] + 2) // 4 % 16
    state = (19, 4, 16, 128)
    rows = (ITEMS, 4, 128)
    face = (10, 24, 128)
    phase, keep, give = call(
        first_kernel, [(4, 16, 128), rows, rows], (fluid, order), [VMEM] * 2, name="moments"
    )
    for step in range(STEPS):
        got = swap("gz", give, 0)
        (pair,) = call(pair_kernel, [(2, *rows)], (keep, got), [VMEM] * 2, name="pair")
        crossed = cross_planes(pair, steps[step])
        other = swap("gz", crossed, 0)
        stack, edge = call(
            stack_kernel,
            [(4, 32, 128), (ITEMS - 3, 8, 128)],
            (phase, crossed, other),
            [VMEM] * 3,
            name="stack",
        )
        wide, one, two = call(
            functools.partial(ghost_kernel, step),
            [(8, 32, 128), (32, 128), (32, 128)],
            (offsets, weights, stack, swap("gx", stack, 0), swap("gx", stack, 1)),
            [SMEM] * 2 + [VMEM] * 3,
            [pltpu.VMEM((12, 32, 128), F32)],
            name="ghosts",
        )
        post, east, west = call(
            collide_kernel,
            [(38, 4, 16, 128), face, face],
            (wide, one, two, swap("gz", one, 0), swap("gz", two, 1), edge, fluid, order),
            [VMEM] * 8,
            [
                pltpu.VMEM((5, 8, 128), F32),
                pltpu.VMEM((8, 32, 128), F32),
                pltpu.VMEM((10, 16, 128), F32),
                pltpu.VMEM((10, 16, 128), F32),
            ],
            name="collide",
        )
        moved, one, two = call(
            functools.partial(stream_kernel, step),
            [(38, 4, 16, 128), (16, 128), (16, 128)],
            (offsets, weights, post, east, swap("gx", east, 0), swap("gx", west, 1)),
            [SMEM] * 2 + [VMEM] * 4,
            [pltpu.VMEM((2, 12, 16, 128), F32)],
            name="stream",
        )
        more = step + 1 < STEPS
        outs = call(
            functools.partial(finish_kernel, more),
            [state, state] + ([(4, 16, 128), rows, rows] if more else []),
            (moved, swap("gz", one, 0), swap("gz", two, 1)),
            [VMEM] * 3,
            name="finish",
        )
        fluid, order = outs[:2]
        if more:
            phase, keep, give = outs[2:]
    return (fluid, order)


def solution(mesh):
    in_specs = (P(None, "gx", "gy", "gz"), P(None, "gx", "gy", "gz"), P(), P())
    out_specs = (P(None, "gx", "gy", "gz"), P(None, "gx", "gy", "gz"))
    return jax.shard_map(
        per_device, mesh=mesh, in_specs=in_specs, out_specs=out_specs, check_vma=False
    )
```

profile of v0, /device:TPU:1, one launch (start us, length us, event | category | flops | bytes accessed | tf_op | source)
XLA Modules:
  0.0 101.5 jit_solution(3590547494877721150)
XLA Ops:
  0.6 0.0 copy-start
  0.6 1.1 %copy-done = f32[19,4,16,128]{3,2,1,0:T(8,128)S(1)} copy-done((f32[19,4,16,128]{3,2,1,0:T(8,128)S(1)}, f32[19,4,16,128]{3,2,1,0:T(8,128)}, u32[]{:S(2)}) %copy-start) | copy-done | bytes 622616
  1.7 1.1 %copy-done.2 = f32[19,4,16,128]{3,2,1,0:T(8,128)S(1)} copy-done((f32[19,4,16,128]{3,2,1,0:T(8,128)S(1)}, f32[19,4,16,128]{3,2,1,0:T(8,128)}, u32[]{:S(2)}) %copy-start.2) | copy-done | bytes 622616
  2.8 0.1 moments.1
  2.9 3.3 %collective-permute-start.32 = (f32[17,4,128]{2,1,0:T(4,128)S(1)}, f32[17,4,128]{2,1,0:T(4,128)S(1)}, u32[]{:S(2)}, u32[]{:S(2)}) collective-permute-start(f32[17,4,128]{2,1,0:T(4,128)S(1)} %get-tuple-element.100), channel_id=1, source_target_pairs={{0,1},{1,0},{2,3},{3,2},{4,5},{5,4},{6,7},{7,6},{8,9},{9,8},{10,11... | collective-permute-start | bytes 104456 | tf_op jit(solution)/shard_map/ppermute | solution.py:416
  6.3 0.0 copy-done.4
  6.3 0.2 add_reduce_fusion
  6.5 0.6 fusion.1
  7.7 0.0 collective-permute-done.32.got_ref
  7.7 9.4 %conditional.2 = (f32[2,17,4,128]{3,2,1,0:T(4,128)}) conditional(s32[]{:T(128)} %bitcast, f32[2,17,4,128]{3,2,1,0:T(4,128)S(1)} %pair.2, f32[2,17,4,128]{3,2,1,0:T(4,128)S(1)} %pair.2, f32[2,17,4,128]{3,2,1,0:T(4,128)S(1)} %pair.2, f32[2,17,4,128]{3,2,1,0:T(4,128)S(1)} %pair.2, ...), branch_computations={%region_0.1_spmd, %region_1.2_spmd, %region_2.3_spmd, %region_3.4_... | conditional | bytes 278576 | solution.py:440
  7.8 6.3 %collective-permute-start.9 = (f32[2,17,4,128]{3,2,1,0:T(4,128)S(1)}, f32[2,17,4,128]{3,2,1,0:T(4,128)}, u32[]{:S(2)}, u32[]{:S(2)}) collective-permute-start(f32[2,17,4,128]{3,2,1,0:T(4,128)S(1)} %param.9), channel_id=1, source_target_pairs={{0,149},{149,0},{2,151},{151,2},{4,153},{153,4},{6,155},{155,6},{8... | collective-permute-start | bytes 208904 | tf_op jit(solution)/shard_map/cond/branch_9_fun/ppermute | solution.py:438
  14.1 3.0 %collective-permute-done.9 = f32[2,17,4,128]{3,2,1,0:T(4,128)} collective-permute-done((f32[2,17,4,128]{3,2,1,0:T(4,128)S(1)}, f32[2,17,4,128]{3,2,1,0:T(4,128)}, u32[]{:S(2)}, u32[]{:S(2)}) %collective-permute-start.9) | collective-permute-done | bytes 69664 | tf_op jit(solution)/shard_map/cond/branch_9_fun/ppermute | solution.py:438
  17.1 1.2 %collective-permute-start.33 = (f32[2,17,4,128]{3,2,1,0:T(4,128)}, f32[2,17,4,128]{3,2,1,0:T(4,128)S(1)}, u32[]{:S(2)}, u32[]{:S(2)}) collective-permute-start(f32[2,17,4,128]{3,2,1,0:T(4,128)} %get-tuple-element.130.crossed_ref), channel_id=1, source_target_pairs={{0,1},{1,0},{2,3},{3,2},{4,5},{5,4},{6,7},{7,6},{8,9},{9,8},{10,11... | collective-permute-start | bytes 208904 | tf_op jit(solution)/shard_map/ppermute | solution.py:416
  18.3 1.1 %collective-permute-done.33.other_ref = f32[2,17,4,128]{3,2,1,0:T(4,128)S(1)} collective-permute-done((f32[2,17,4,128]{3,2,1,0:T(4,128)}, f32[2,17,4,128]{3,2,1,0:T(4,128)S(1)}, u32[]{:S(2)}, u32[]{:S(2)}) %collective-permute-start.33) | collective-permute-done | bytes 69664 | tf_op jit(solution)/shard_map/ppermute | solution.py:416
  19.5 0.9 stack.2
  20.4 7.2 %collective-permute-start.35 = (f32[4,32,128]{2,1,0:T(8,128)S(1)}, f32[4,32,128]{2,1,0:T(8,128)S(1)}, u32[]{:S(2)}, u32[]{:S(2)}) collective-permute-start(f32[4,32,128]{2,1,0:T(8,128)S(1)} %get-tuple-element.101.own_ref), channel_id=1, source_target_pairs={{16,32},{32,16},{48,64},{64,48},{80,96},{96,80},{112,128},{128,112... | collective-permute-start | bytes 196616 | tf_op jit(solution)/shard_map/ppermute | solution.py:416
  27.5 0.0 collective-permute-start.34
  27.6 2.4 %collective-permute-done.35.two_ref = f32[4,32,128]{2,1,0:T(8,128)S(1)} collective-permute-done((f32[4,32,128]{2,1,0:T(8,128)S(1)}, f32[4,32,128]{2,1,0:T(8,128)S(1)}, u32[]{:S(2)}, u32[]{:S(2)}) %collective-permute-start.35) | collective-permute-done | bytes 65568 | tf_op jit(solution)/shard_map/ppermute | solution.py:416
  29.9 1.0 %collective-permute-done.34.one_ref = f32[4,32,128]{2,1,0:T(8,128)S(1)} collective-permute-done((f32[4,32,128]{2,1,0:T(8,128)S(1)}, f32[4,32,128]{2,1,0:T(8,128)S(1)}, u32[]{:S(2)}, u32[]{:S(2)}) %collective-permute-start.34) | collective-permute-done | bytes 65568 | tf_op jit(solution)/shard_map/ppermute | solution.py:416
  31.0 0.7 ghosts.2
  31.7 1.6 %collective-permute-start.36 = (f32[32,128]{1,0:T(8,128)S(1)}, f32[32,128]{1,0:T(8,128)S(1)}, u32[]{:S(2)}, u32[]{:S(2)}) collective-permute-start(f32[32,128]{1,0:T(8,128)S(1)} %get-tuple-element.103.sent_one), channel_id=1, source_target_pairs={{0,1},{1,0},{2,3},{3,2},{4,5},{5,4},{6,7},{7,6},{8,9},{9,8},{10,11... | collective-permute-start | bytes 49160 | tf_op jit(solution)/shard_map/ppermute | solution.py:416
  33.2 0.7 collective-permute-start.37
  34.0 0.1 collective-permute-done.36.got_one
  34.1 2.3 %collective-permute-done.37.got_two = f32[32,128]{1,0:T(8,128)S(1)} collective-permute-done((f32[32,128]{1,0:T(8,128)S(1)}, f32[32,128]{1,0:T(8,128)S(1)}, u32[]{:S(2)}, u32[]{:S(2)}) %collective-permute-start.37) | collective-permute-done | bytes 16416 | tf_op jit(solution)/shard_map/ppermute | solution.py:416
  36.4 0.0 copy-done.1
  36.4 0.6 collide.2
  37.0 5.5 %collective-permute-start.39 = (f32[10,24,128]{2,1,0:T(8,128)S(1)}, f32[10,24,128]{2,1,0:T(8,128)S(1)}, u32[]{:S(2)}, u32[]{:S(2)}) collective-permute-start(f32[10,24,128]{2,1,0:T(8,128)S(1)} %get-tuple-element.108), channel_id=1, source_target_pairs={{16,32},{32,16},{48,64},{64,48},{80,96},{96,80},{112,128},{128,112... | collective-permute-start | bytes 368648 | tf_op jit(solution)/shard_map/ppermute | solution.py:416
  42.6 0.0 collective-permute-start.38
  42.6 5.2 %collective-permute-done.39.two_ref = f32[10,24,128]{2,1,0:T(8,128)S(1)} collective-permute-done((f32[10,24,128]{2,1,0:T(8,128)S(1)}, f32[10,24,128]{2,1,0:T(8,128)S(1)}, u32[]{:S(2)}, u32[]{:S(2)}) %collective-permute-start.39) | collective-permute-done | bytes 122912 | tf_op jit(solution)/shard_map/ppermute | solution.py:416
  47.7 0.0 collective-permute-done.38.one_ref
  47.7 0.9 stream.2
  48.6 1.0 %collective-permute-start.40 = (f32[16,128]{1,0:T(8,128)S(1)}, f32[16,128]{1,0:T(8,128)S(1)}, u32[]{:S(2)}, u32[]{:S(2)}) collective-permute-start(f32[16,128]{1,0:T(8,128)S(1)} %get-tuple-element.110), channel_id=1, source_target_pairs={{0,1},{1,0},{2,3},{3,2},{4,5},{5,4},{6,7},{7,6},{8,9},{9,8},{10,11... | collective-permute-start | bytes 24584 | tf_op jit(solution)/shard_map/ppermute | solution.py:416
  49.6 1.8 %collective-permute-start.41 = (f32[16,128]{1,0:T(8,128)S(1)}, f32[16,128]{1,0:T(8,128)S(1)}, u32[]{:S(2)}, u32[]{:S(2)}) collective-permute-start(f32[16,128]{1,0:T(8,128)S(1)} %get-tuple-element.111), channel_id=1, source_target_pairs={{1,2},{2,1},{3,0},{0,3},{5,6},{6,5},{7,4},{4,7},{9,10},{10,9},{11,... | collective-permute-start | bytes 24584 | tf_op jit(solution)/shard_map/ppermute | solution.py:416
  51.4 0.0 collective-permute-done.40.one_ref
  51.4 1.3 %collective-permute-done.41.two_ref = f32[16,128]{1,0:T(8,128)S(1)} collective-permute-done((f32[16,128]{1,0:T(8,128)S(1)}, f32[16,128]{1,0:T(8,128)S(1)}, u32[]{:S(2)}, u32[]{:S(2)}) %collective-permute-start.41) | collective-permute-done | bytes 8224 | tf_op jit(solution)/shard_map/ppermute | solution.py:416
  52.7 0.4 finish.2
  53.1 0.5 collective-permute-start.42
  54.3 0.2 collective-permute-done.42.got_ref
  54.6 7.8 %conditional.3 = (f32[2,17,4,128]{3,2,1,0:T(4,128)}) conditional(s32[]{:T(128)} %bitcast.1, f32[2,17,4,128]{3,2,1,0:T(4,128)S(1)} %pair.3, f32[2,17,4,128]{3,2,1,0:T(4,128)S(1)} %pair.3, f32[2,17,4,128]{3,2,1,0:T(4,128)S(1)} %pair.3, f32[2,17,4,128]{3,2,1,0:T(4,128)S(1)} %pair.3, ...), branch_computations={%region_16.17_spmd, %region_17.18_spmd, %region_18.19_spmd, %regio... | conditional | bytes 278576 | solution.py:440
  54.6 0.0 collective-permute-start.27
  54.6 7.7 %collective-permute-done.27 = f32[2,17,4,128]{3,2,1,0:T(4,128)} collective-permute-done((f32[2,17,4,128]{3,2,1,0:T(4,128)S(1)}, f32[2,17,4,128]{3,2,1,0:T(4,128)}, u32[]{:S(2)}, u32[]{:S(2)}) %collective-permute-start.27) | collective-permute-done | bytes 69664 | tf_op jit(solution)/shard_map/cond/branch_11_fun/ppermute | solution.py:438
  62.3 1.9 %collective-permute-start.43 = (f32[2,17,4,128]{3,2,1,0:T(4,128)}, f32[2,17,4,128]{3,2,1,0:T(4,128)S(1)}, u32[]{:S(2)}, u32[]{:S(2)}) collective-permute-start(f32[2,17,4,128]{3,2,1,0:T(4,128)} %get-tuple-element.131.crossed_ref), channel_id=1, source_target_pairs={{0,1},{1,0},{2,3},{3,2},{4,5},{5,4},{6,7},{7,6},{8,9},{9,8},{10,11... | collective-permute-start | bytes 208904 | tf_op jit(solution)/shard_map/ppermute | solution.py:416
  64.2 1.1 %collective-permute-done.43.other_ref = f32[2,17,4,128]{3,2,1,0:T(4,128)S(1)} collective-permute-done((f32[2,17,4,128]{3,2,1,0:T(4,128)}, f32[2,17,4,128]{3,2,1,0:T(4,128)S(1)}, u32[]{:S(2)}, u32[]{:S(2)}) %collective-permute-start.43) | collective-permute-done | bytes 69664 | tf_op jit(solution)/shard_map/ppermute | solution.py:416
  65.3 0.9 stack.3
  66.2 9.1 %collective-permute-start.45 = (f32[4,32,128]{2,1,0:T(8,128)S(1)}, f32[4,32,128]{2,1,0:T(8,128)S(1)}, u32[]{:S(2)}, u32[]{:S(2)}) collective-permute-start(f32[4,32,128]{2,1,0:T(8,128)S(1)} %get-tuple-element.115.own_ref), channel_id=1, source_target_pairs={{16,32},{32,16},{48,64},{64,48},{80,96},{96,80},{112,128},{128,112... | collective-permute-start | bytes 196616 | tf_op jit(solution)/shard_map/ppermute | solution.py:416
  75.3 0.0 collective-permute-start.44
  75.3 2.6 %collective-permute-done.45.two_ref = f32[4,32,128]{2,1,0:T(8,128)S(1)} collective-permute-done((f32[4,32,128]{2,1,0:T(8,128)S(1)}, f32[4,32,128]{2,1,0:T(8,128)S(1)}, u32[]{:S(2)}, u32[]{:S(2)}) %collective-permute-start.45) | collective-permute-done | bytes 65568 | tf_op jit(solution)/shard_map/ppermute | solution.py:416
  77.9 0.5 collective-permute-done.44.one_ref
  78.4 0.7 ghosts.3
  79.1 1.7 %collective-permute-start.46 = (f32[32,128]{1,0:T(8,128)S(1)}, f32[32,128]{1,0:T(8,128)S(1)}, u32[]{:S(2)}, u32[]{:S(2)}) collective-permute-start(f32[32,128]{1,0:T(8,128)S(1)} %get-tuple-element.117.sent_one), channel_id=1, source_target_pairs={{0,1},{1,0},{2,3},{3,2},{4,5},{5,4},{6,7},{7,6},{8,9},{9,8},{10,11... | collective-permute-start | bytes 49160 | tf_op jit(solution)/shard_map/ppermute | solution.py:416
  80.8 0.0 collective-permute-start.47
  80.8 0.8 collective-permute-done.46.got_one
  81.6 2.3 %collective-permute-done.47.got_two = f32[32,128]{1,0:T(8,128)S(1)} collective-permute-done((f32[32,128]{1,0:T(8,128)S(1)}, f32[32,128]{1,0:T(8,128)S(1)}, u32[]{:S(2)}, u32[]{:S(2)}) %collective-permute-start.47) | collective-permute-done | bytes 16416 | tf_op jit(solution)/shard_map/ppermute | solution.py:416
  84.0 0.6 collide.3
  84.6 5.1 %collective-permute-start.49 = (f32[10,24,128]{2,1,0:T(8,128)S(1)}, f32[10,24,128]{2,1,0:T(8,128)S(1)}, u32[]{:S(2)}, u32[]{:S(2)}) collective-permute-start(f32[10,24,128]{2,1,0:T(8,128)S(1)} %get-tuple-element.124), channel_id=1, source_target_pairs={{16,32},{32,16},{48,64},{64,48},{80,96},{96,80},{112,128},{128,112... | collective-permute-start | bytes 368648 | tf_op jit(solution)/shard_map/ppermute | solution.py:416
  89.7 0.0 collective-permute-start.48
  89.7 5.4 %collective-permute-done.49.two_ref = f32[10,24,128]{2,1,0:T(8,128)S(1)} collective-permute-done((f32[10,24,128]{2,1,0:T(8,128)S(1)}, f32[10,24,128]{2,1,0:T(8,128)S(1)}, u32[]{:S(2)}, u32[]{:S(2)}) %collective-permute-start.49) | collective-permute-done | bytes 122912 | tf_op jit(solution)/shard_map/ppermute | solution.py:416
  95.1 0.0 collective-permute-done.48.one_ref
  95.1 0.9 stream.3
  96.0 0.8 collective-permute-start.50
  96.8 2.0 %collective-permute-start.51 = (f32[16,128]{1,0:T(8,128)S(1)}, f32[16,128]{1,0:T(8,128)S(1)}, u32[]{:S(2)}, u32[]{:S(2)}) collective-permute-start(f32[16,128]{1,0:T(8,128)S(1)} %get-tuple-element.127), channel_id=1, source_target_pairs={{1,2},{2,1},{3,0},{0,3},{5,6},{6,5},{7,4},{4,7},{9,10},{10,9},{11,... | collective-permute-start | bytes 24584 | tf_op jit(solution)/shard_map/ppermute | solution.py:416
  98.8 0.0 collective-permute-done.50.one_ref
  98.8 1.3 %collective-permute-done.51.two_ref = f32[16,128]{1,0:T(8,128)S(1)} collective-permute-done((f32[16,128]{1,0:T(8,128)S(1)}, f32[16,128]{1,0:T(8,128)S(1)}, u32[]{:S(2)}, u32[]{:S(2)}) %collective-permute-start.51) | collective-permute-done | bytes 8224 | tf_op jit(solution)/shard_map/ppermute | solution.py:416
  100.1 1.4 %finish.3 = (f32[19,4,16,128]{3,2,1,0:T(8,128)}, f32[19,4,16,128]{3,2,1,0:T(8,128)}) custom-call(f32[38,4,16,128]{3,2,1,0:T(8,128)S(1)} %get-tuple-element.125.moved_ref, f32[16,128]{1,0:T(8,128)S(1)} %collective-permute-done.50.one_ref, f32[16,128]{1,0:T(8,128)S(1)} %collective-permute-done.51.two_ref), custom_call_target="tpu_custom_call" | custom-call | tf_op jit(solution)/shard_map/finish/pallas_call | solution.py:59
  (10 shorter events, 0.0 us)
Async XLA Ops:
  0.6 1.1 %copy-start = (f32[19,4,16,128]{3,2,1,0:T(8,128)S(1)}, f32[19,4,16,128]{3,2,1,0:T(8,128)}, u32[]{:S(2)}) copy-start(f32[19,4,16,128]{3,2,1,0:T(8,128)} %f_ref.3) | copy-start | bytes 1867780
  1.7 1.1 %copy-start.2 = (f32[19,4,16,128]{3,2,1,0:T(8,128)S(1)}, f32[19,4,16,128]{3,2,1,0:T(8,128)}, u32[]{:S(2)}) copy-start(f32[19,4,16,128]{3,2,1,0:T(8,128)} %g_ref.3) | copy-start | bytes 1867780
  2.8 3.5 %copy-start.4 = (s32[2,4]{1,0:T(2,128)S(1)}, s32[2,4]{1,0:T(2,128)}, u32[]{:S(2)}) copy-start(s32[2,4]{1,0:T(2,128)} %offsets.7) | copy-start | bytes 100
  2.8 28.2 %copy-start.5 = (f32[4]{0:T(128)S(1)}, f32[4]{0:T(128)}, u32[]{:S(2)}) copy-start(f32[4]{0:T(128)} %weights.7) | copy-start | bytes 52
  2.8 33.6 %copy-start.1 = (f32[19,4,16,128]{3,2,1,0:T(8,128)S(1)}, f32[19,4,16,128]{3,2,1,0:T(8,128)}, u32[]{:S(2)}) copy-start(f32[19,4,16,128]{3,2,1,0:T(8,128)} %f_ref.3) | copy-start | bytes 1867780
  2.8 33.6 %copy-start.3 = (f32[19,4,16,128]{3,2,1,0:T(8,128)S(1)}, f32[19,4,16,128]{3,2,1,0:T(8,128)}, u32[]{:S(2)}) copy-start(f32[19,4,16,128]{3,2,1,0:T(8,128)} %g_ref.3) | copy-start | bytes 1867780
  2.9 4.8 %collective-permute-start.32 = (f32[17,4,128]{2,1,0:T(4,128)S(1)}, f32[17,4,128]{2,1,0:T(4,128)S(1)}, u32[]{:S(2)}, u32[]{:S(2)}) collective-permute-start(f32[17,4,128]{2,1,0:T(4,128)S(1)} %get-tuple-element.100), channel_id=1, source_target_pairs={{0,1},{1,0},{2,3},{3,2},{4,5},{5,4},{6,7},{7,6},{8,9},{9,8},{10,11... | collective-permute-start | bytes 104456 | tf_op jit(solution)/shard_map/ppermute | solution.py:416
  7.8 9.4 %collective-permute-start.9 = (f32[2,17,4,128]{3,2,1,0:T(4,128)S(1)}, f32[2,17,4,128]{3,2,1,0:T(4,128)}, u32[]{:S(2)}, u32[]{:S(2)}) collective-permute-start(f32[2,17,4,128]{3,2,1,0:T(4,128)S(1)} %param.9), channel_id=1, source_target_pairs={{0,149},{149,0},{2,151},{151,2},{4,153},{153,4},{6,155},{155,6},{8... | collective-permute-start | bytes 208904 | tf_op jit(solution)/shard_map/cond/branch_9_fun/ppermute | solution.py:438
  17.1 2.4 %collective-permute-start.33 = (f32[2,17,4,128]{3,2,1,0:T(4,128)}, f32[2,17,4,128]{3,2,1,0:T(4,128)S(1)}, u32[]{:S(2)}, u32[]{:S(2)}) collective-permute-start(f32[2,17,4,128]{3,2,1,0:T(4,128)} %get-tuple-element.130.crossed_ref), channel_id=1, source_target_pairs={{0,1},{1,0},{2,3},{3,2},{4,5},{5,4},{6,7},{7,6},{8,9},{9,8},{10,11... | collective-permute-start | bytes 208904 | tf_op jit(solution)/shard_map/ppermute | solution.py:416
  20.4 9.5 %collective-permute-start.35 = (f32[4,32,128]{2,1,0:T(8,128)S(1)}, f32[4,32,128]{2,1,0:T(8,128)S(1)}, u32[]{:S(2)}, u32[]{:S(2)}) collective-permute-start(f32[4,32,128]{2,1,0:T(8,128)S(1)} %get-tuple-element.101.own_ref), channel_id=1, source_target_pairs={{16,32},{32,16},{48,64},{64,48},{80,96},{96,80},{112,128},{128,112... | collective-permute-start | bytes 196616 | tf_op jit(solution)/shard_map/ppermute | solution.py:416
  27.5 3.4 %collective-permute-start.34 = (f32[4,32,128]{2,1,0:T(8,128)S(1)}, f32[4,32,128]{2,1,0:T(8,128)S(1)}, u32[]{:S(2)}, u32[]{:S(2)}) collective-permute-start(f32[4,32,128]{2,1,0:T(8,128)S(1)} %get-tuple-element.101.own_ref), channel_id=1, source_target_pairs={{0,16},{16,0},{32,48},{48,32},{64,80},{80,64},{96,112},{112,96},{1... | collective-permute-start | bytes 196616 | tf_op jit(solution)/shard_map/ppermute | solution.py:416
  31.7 2.4 %collective-permute-start.36 = (f32[32,128]{1,0:T(8,128)S(1)}, f32[32,128]{1,0:T(8,128)S(1)}, u32[]{:S(2)}, u32[]{:S(2)}) collective-permute-start(f32[32,128]{1,0:T(8,128)S(1)} %get-tuple-element.103.sent_one), channel_id=1, source_target_pairs={{0,1},{1,0},{2,3},{3,2},{4,5},{5,4},{6,7},{7,6},{8,9},{9,8},{10,11... | collective-permute-start | bytes 49160 | tf_op jit(solution)/shard_map/ppermute | solution.py:416
  33.2 3.2 %collective-permute-start.37 = (f32[32,128]{1,0:T(8,128)S(1)}, f32[32,128]{1,0:T(8,128)S(1)}, u32[]{:S(2)}, u32[]{:S(2)}) collective-permute-start(f32[32,128]{1,0:T(8,128)S(1)} %get-tuple-element.104.sent_two), channel_id=1, source_target_pairs={{1,2},{2,1},{3,0},{0,3},{5,6},{6,5},{7,4},{4,7},{9,10},{10,9},{11,... | collective-permute-start | bytes 49160 | tf_op jit(solution)/shard_map/ppermute | solution.py:416
  37.0 10.7 %collective-permute-start.39 = (f32[10,24,128]{2,1,0:T(8,128)S(1)}, f32[10,24,128]{2,1,0:T(8,128)S(1)}, u32[]{:S(2)}, u32[]{:S(2)}) collective-permute-start(f32[10,24,128]{2,1,0:T(8,128)S(1)} %get-tuple-element.108), channel_id=1, source_target_pairs={{16,32},{32,16},{48,64},{64,48},{80,96},{96,80},{112,128},{128,112... | collective-permute-start | bytes 368648 | tf_op jit(solution)/shard_map/ppermute | solution.py:416
  42.6 5.2 %collective-permute-start.38 = (f32[10,24,128]{2,1,0:T(8,128)S(1)}, f32[10,24,128]{2,1,0:T(8,128)S(1)}, u32[]{:S(2)}, u32[]{:S(2)}) collective-permute-start(f32[10,24,128]{2,1,0:T(8,128)S(1)} %get-tuple-element.107.own_ref), channel_id=1, source_target_pairs={{0,16},{16,0},{32,48},{48,32},{64,80},{80,64},{96,112},{112,96},{1... | collective-permute-start | bytes 368648 | tf_op jit(solution)/shard_map/ppermute | solution.py:416
  48.6 2.8 %collective-permute-start.40 = (f32[16,128]{1,0:T(8,128)S(1)}, f32[16,128]{1,0:T(8,128)S(1)}, u32[]{:S(2)}, u32[]{:S(2)}) collective-permute-start(f32[16,128]{1,0:T(8,128)S(1)} %get-tuple-element.110), channel_id=1, source_target_pairs={{0,1},{1,0},{2,3},{3,2},{4,5},{5,4},{6,7},{7,6},{8,9},{9,8},{10,11... | collective-permute-start | bytes 24584 | tf_op jit(solution)/shard_map/ppermute | solution.py:416
  49.6 3.1 %collective-permute-start.41 = (f32[16,128]{1,0:T(8,128)S(1)}, f32[16,128]{1,0:T(8,128)S(1)}, u32[]{:S(2)}, u32[]{:S(2)}) collective-permute-start(f32[16,128]{1,0:T(8,128)S(1)} %get-tuple-element.111), channel_id=1, source_target_pairs={{1,2},{2,1},{3,0},{0,3},{5,6},{6,5},{7,4},{4,7},{9,10},{10,9},{11,... | collective-permute-start | bytes 24584 | tf_op jit(solution)/shard_map/ppermute | solution.py:416
  53.1 1.4 %collective-permute-start.42 = (f32[17,4,128]{2,1,0:T(4,128)S(1)}, f32[17,4,128]{2,1,0:T(4,128)S(1)}, u32[]{:S(2)}, u32[]{:S(2)}) collective-permute-start(f32[17,4,128]{2,1,0:T(4,128)S(1)} %get-tuple-element.114), channel_id=1, source_target_pairs={{0,1},{1,0},{2,3},{3,2},{4,5},{5,4},{6,7},{7,6},{8,9},{9,8},{10,11... | collective-permute-start | bytes 104456 | tf_op jit(solution)/shard_map/ppermute | solution.py:416
  54.6 7.8 %collective-permute-start.27 = (f32[2,17,4,128]{3,2,1,0:T(4,128)S(1)}, f32[2,17,4,128]{3,2,1,0:T(4,128)}, u32[]{:S(2)}, u32[]{:S(2)}) collective-permute-start(f32[2,17,4,128]{3,2,1,0:T(4,128)S(1)} %param.27), channel_id=1, source_target_pairs={{0,181},{181,0},{2,183},{183,2},{4,185},{185,4},{6,187},{187,6},{8... | collective-permute-start | bytes 208904 | tf_op jit(solution)/shard_map/cond/branch_11_fun/ppermute | solution.py:438
  62.3 3.0 %collective-permute-start.43 = (f32[2,17,4,128]{3,2,1,0:T(4,128)}, f32[2,17,4,128]{3,2,1,0:T(4,128)S(1)}, u32[]{:S(2)}, u32[]{:S(2)}) collective-permute-start(f32[2,17,4,128]{3,2,1,0:T(4,128)} %get-tuple-element.131.crossed_ref), channel_id=1, source_target_pairs={{0,1},{1,0},{2,3},{3,2},{4,5},{5,4},{6,7},{7,6},{8,9},{9,8},{10,11... | collective-permute-start | bytes 208904 | tf_op jit(solution)/shard_map/ppermute | solution.py:416
  66.2 11.7 %collective-permute-start.45 = (f32[4,32,128]{2,1,0:T(8,128)S(1)}, f32[4,32,128]{2,1,0:T(8,128)S(1)}, u32[]{:S(2)}, u32[]{:S(2)}) collective-permute-start(f32[4,32,128]{2,1,0:T(8,128)S(1)} %get-tuple-element.115.own_ref), channel_id=1, source_target_pairs={{16,32},{32,16},{48,64},{64,48},{80,96},{96,80},{112,128},{128,112... | collective-permute-start | bytes 196616 | tf_op jit(solution)/shard_map/ppermute | solution.py:416
  75.3 3.1 %collective-permute-start.44 = (f32[4,32,128]{2,1,0:T(8,128)S(1)}, f32[4,32,128]{2,1,0:T(8,128)S(1)}, u32[]{:S(2)}, u32[]{:S(2)}) collective-permute-start(f32[4,32,128]{2,1,0:T(8,128)S(1)} %get-tuple-element.115.own_ref), channel_id=1, source_target_pairs={{0,16},{16,0},{32,48},{48,32},{64,80},{80,64},{96,112},{112,96},{1... | collective-permute-start | bytes 196616 | tf_op jit(solution)/shard_map/ppermute | solution.py:416
  79.1 2.5 %collective-permute-start.46 = (f32[32,128]{1,0:T(8,128)S(1)}, f32[32,128]{1,0:T(8,128)S(1)}, u32[]{:S(2)}, u32[]{:S(2)}) collective-permute-start(f32[32,128]{1,0:T(8,128)S(1)} %get-tuple-element.117.sent_one), channel_id=1, source_target_pairs={{0,1},{1,0},{2,3},{3,2},{4,5},{5,4},{6,7},{7,6},{8,9},{9,8},{10,11... | collective-permute-start | bytes 49160 | tf_op jit(solution)/shard_map/ppermute | solution.py:416
  80.8 3.2 %collective-permute-start.47 = (f32[32,128]{1,0:T(8,128)S(1)}, f32[32,128]{1,0:T(8,128)S(1)}, u32[]{:S(2)}, u32[]{:S(2)}) collective-permute-start(f32[32,128]{1,0:T(8,128)S(1)} %get-tuple-element.118.sent_two), channel_id=1, source_target_pairs={{1,2},{2,1},{3,0},{0,3},{5,6},{6,5},{7,4},{4,7},{9,10},{10,9},{11,... | collective-permute-start | bytes 49160 | tf_op jit(solution)/shard_map/ppermute | solution.py:416
  84.6 10.5 %collective-permute-start.49 = (f32[10,24,128]{2,1,0:T(8,128)S(1)}, f32[10,24,128]{2,1,0:T(8,128)S(1)}, u32[]{:S(2)}, u32[]{:S(2)}) collective-permute-start(f32[10,24,128]{2,1,0:T(8,128)S(1)} %get-tuple-element.124), channel_id=1, source_target_pairs={{16,32},{32,16},{48,64},{64,48},{80,96},{96,80},{112,128},{128,112... | collective-permute-start | bytes 368648 | tf_op jit(solution)/shard_map/ppermute | solution.py:416
  89.7 5.4 %collective-permute-start.48 = (f32[10,24,128]{2,1,0:T(8,128)S(1)}, f32[10,24,128]{2,1,0:T(8,128)S(1)}, u32[]{:S(2)}, u32[]{:S(2)}) collective-permute-start(f32[10,24,128]{2,1,0:T(8,128)S(1)} %get-tuple-element.123.own_ref), channel_id=1, source_target_pairs={{0,16},{16,0},{32,48},{48,32},{64,80},{80,64},{96,112},{112,96},{1... | collective-permute-start | bytes 368648 | tf_op jit(solution)/shard_map/ppermute | solution.py:416
  96.0 2.8 %collective-permute-start.50 = (f32[16,128]{1,0:T(8,128)S(1)}, f32[16,128]{1,0:T(8,128)S(1)}, u32[]{:S(2)}, u32[]{:S(2)}) collective-permute-start(f32[16,128]{1,0:T(8,128)S(1)} %get-tuple-element.126), channel_id=1, source_target_pairs={{0,1},{1,0},{2,3},{3,2},{4,5},{5,4},{6,7},{7,6},{8,9},{9,8},{10,11... | collective-permute-start | bytes 24584 | tf_op jit(solution)/shard_map/ppermute | solution.py:416
  96.8 3.3 %collective-permute-start.51 = (f32[16,128]{1,0:T(8,128)S(1)}, f32[16,128]{1,0:T(8,128)S(1)}, u32[]{:S(2)}, u32[]{:S(2)}) collective-permute-start(f32[16,128]{1,0:T(8,128)S(1)} %get-tuple-element.127), channel_id=1, source_target_pairs={{1,2},{2,1},{3,0},{0,3},{5,6},{6,5},{7,4},{4,7},{9,10},{10,9},{11,... | collective-permute-start | bytes 24584 | tf_op jit(solution)/shard_map/ppermute | solution.py:416
where the time goes:
time: 101 us; the launch traced here: 102 us
  starting transfers between devices  49.8 us (49%)
  waiting for transfers between devices  38.7 us (38%)
  Pallas kernels  8.06 us (8%)
  local copies, waits for them, and re-layouts  2.75 us (3%)
  between operations  2.05 us (2%)
    ppermute x20, starting transfers between devices, swap(): return lax.ppermute(values, axis, pairs)  43.4 us
    ppermute x20, waiting for transfers between devices, swap(): return lax.ppermute(values, axis, pairs)  27.9 us
    ppermute x2, waiting for transfers between devices, branch(): return lambda sent: lax.ppermute(sent, axes, pairs)  10.8 us
    pallas_call x13, Pallas kernels, call(): pl.pallas_call(body, out_shape=[jax.ShapeDtypeStruct(shape, F32) for shap...  8.06 us
    ppermute x2, starting transfers between devices, branch(): return lambda sent: lax.ppermute(sent, axes, pairs)  6.33 us
    unnamed x12, local copies, waits for them, and re-layouts  2.16 us
  transfers between devices with their start and end apart: 22, of which 17 were waited for; matrix products, arithmetic and copies ran while one was open for 1% of the time, Pallas kernels for 0%

commit v1 on v0

--- a/solution.py
+++ b/solution.py
@@ -50,6 +50,12 @@
 ABOVE_EDGE = 28
 ITEMS = 17
 
+REACH = [(k, side, (1 - 2 * side) * VELOCITIES[RISING[k % 5]][0]) for k in range(10) for side in (0, 1)]
+FROM_WEST = [(k, side, place) for k, side, cx in REACH for place in range(2 - cx, 4)]
+FROM_EAST = [(k, side, place) for k, side, cx in REACH for place in range(8, 10 - cx)]
+GHOSTS = 160
+FAR = (1, 2, 8, 9, 22, 23, 28, 29)
+
 VMEM = pl.BlockSpec(memory_space=pltpu.VMEM)
 SMEM = pl.BlockSpec(memory_space=pltpu.SMEM)
 F32 = jnp.float32
@@ -133,20 +139,30 @@
     pair_ref[1] = got_ref[...]
 
 
-def stack_kernel(phase_ref, crossed_ref, other_ref, stack_ref, edge_ref):
+def stack_kernel(phase_ref, crossed_ref, other_ref, stack_ref, edge_ref, send_one, send_two):
     odd = is_odd("gz")
-    stack_ref[...] = jnp.zeros_like(stack_ref)
     for x in range(4):
+        stack_ref[x, 0:8, :] = jnp.zeros((8, 128), F32)
         stack_ref[x, OWN : OWN + 16, :] = phase_ref[x]
     for item in range(ITEMS):
         above, below = swapped(odd, crossed_ref[1, item], other_ref[0, item])
         if item < 3:
             for x in range(4):
                 stack_ref[x, item : item + 1, :] = below[x : x + 1]
-                stack_ref[x, ABOVE_EDGE + item : ABOVE_EDGE + item + 1, :] = above[x : x + 1]
+                stack_ref[x, 3 + item : 4 + item, :] = above[x : x + 1]
         else:
             edge_ref[item - 3, 0:4, :] = below
             edge_ref[item - 3, 4:8, :] = above
+    odd = is_odd("gx")
+    for n in range(2):
+        rows = slice(24 * n, 24 * n + 24)
+        send_one[rows, :], send_two[rows, :] = swapped(odd, stack_ref[3 - n], stack_ref[n])
+    for n, row in enumerate(FAR):
+        row = row - 25 if row >= ABOVE_EDGE else row
+        at = slice(48 + n, 49 + n)
+        send_one[at, :], send_two[at, :] = swapped(
+            odd, stack_ref[1, row : row + 1, :], stack_ref[2, row : row + 1, :]
+        )
 
 
 def ghost_kernel(
@@ -158,11 +174,24 @@
     w_down = weights[down]
     w_up = weights[up]
     odd = is_odd("gx")
-    wide[4:8] = own_ref[...]
+
+    def place_cell(place, value):
+        wide[place, 0:24, :] = value
+        wide[place, 24:32, :] = jnp.zeros((8, 128), F32)
+        wide[place, ABOVE_EDGE : ABOVE_EDGE + 3, :] = value[3:6]
+
     for x in range(4):
-        east, west = swapped(odd, one_ref[x], two_ref[x])
-        wide[x] = west
-        wide[8 + x] = east
+        place_cell(4 + x, own_ref[x])
+    for n in range(2):
+        rows = slice(24 * n, 24 * n + 24)
+        east, west = swapped(odd, one_ref[rows, :], two_ref[rows, :])
+        place_cell(3 - n, west)
+        place_cell(8 + n, east)
+    east, west = swapped(odd, one_ref[48:56, :], two_ref[48:56, :])
+    for place, value in ((1, west), (10, east)):
+        wide[place] = jnp.zeros((32, 128), F32)
+        for n, row_number in enumerate(FAR):
+            wide[place, row_number : row_number + 1, :] = value[n : n + 1]
     shape = (32, 128)
     row = rows_of(shape)
     lane = lanes(shape)
@@ -203,6 +232,7 @@
     f_ref,
     g_ref,
     post_ref,
+    edges_ref,
     send_one,
     send_two,
     ghost,
@@ -312,12 +342,19 @@
         fs = fs - (3.0 * WEIGHTS[i] * VELOCITIES[i][0] * U) * density
         geq = WEIGHTS[i] * (3.0 * M * pot + 3.0 * phase * flow)
         gs = (1.0 - 1.0 / TAU_G) * edge_ref[9 + k] + (1.0 / TAU_G) * geq
-        for ref in (send_one, send_two):
-            ref[k, 16:24, :] = fs
-            ref[5 + k, 16:24, :] = gs
+        edges_ref[k] = fs
+        edges_ref[5 + k] = gs
     odd = is_odd("gx")
     for k in range(10):
-        send_one[k, 0:16, :], send_two[k, 0:16, :] = swapped(odd, east[k], west[k])
+        rows = slice(16 * k, 16 * k + 16)
+        send_one[rows, :], send_two[rows, :] = swapped(odd, east[k], west[k])
+    for n, (to_east, to_west) in enumerate(zip(FROM_WEST, FROM_EAST)):
+        values = []
+        for k, side, place in (to_east, to_west):
+            at = 4 * side + place % 4
+            values.append(edges_ref[k, at : at + 1, :])
+        at = slice(GHOSTS + n, GHOSTS + n + 1)
+        send_one[at, :], send_two[at, :] = swapped(odd, *values)
 
 
 def directed(velocity, parts):
@@ -340,12 +377,16 @@
     w_up = weights[up]
     odd = is_odd("gx")
     for k in range(10):
-        from_east, from_west = swapped(odd, one_ref[k, 16:24, :], two_ref[k, 16:24, :])
-        for place, rows in enumerate((from_west, own_ref[k, 16:24, :], from_east)):
-            for side in (0, 1):
-                for x in range(4):
-                    at = 4 * side + x
-                    wide[side, 4 * place + x, k : k + 1, :] = rows[at : at + 1]
+        for side in (0, 1):
+            for x in range(4):
+                at = 4 * side + x
+                wide[side, 4 + x, k : k + 1, :] = own_ref[k, at : at + 1, :]
+    for first in range(0, len(FROM_WEST), 8):
+        rows = slice(GHOSTS + first, GHOSTS + first + 8)
+        from_east, from_west = swapped(odd, one_ref[rows, :], two_ref[rows, :])
+        for value, table in ((from_east, FROM_EAST), (from_west, FROM_WEST)):
+            for n, (k, side, place) in enumerate(table[first : first + 8]):
+                wide[side, place, k : k + 1, :] = value[n : n + 1]
     shape = (16, 128)
     row = rows_of(shape)
     lane = lanes(shape)
@@ -366,10 +407,12 @@
             source = x - cx
             if source < 0:
                 k = 5 * part + EAST.index(component)
-                value = jnp.where(odd, one_ref[k, 0:16, :], two_ref[k, 0:16, :])
+                rows = slice(16 * k, 16 * k + 16)
+                value = jnp.where(odd, one_ref[rows, :], two_ref[rows, :])
             elif source > 3:
                 k = 5 * part + WEST.index(component)
-                value = jnp.where(odd, two_ref[k, 0:16, :], one_ref[k, 0:16, :])
+                rows = slice(16 * k, 16 * k + 16)
+                value = jnp.where(odd, two_ref[rows, :], one_ref[rows, :])
             else:
                 value = post_ref[i, source]
             if cy == 1:
@@ -445,7 +488,7 @@
     steps = (offsets[:, plane] + 2) // 4 % 16
     state = (19, 4, 16, 128)
     rows = (ITEMS, 4, 128)
-    face = (10, 24, 128)
+    face = (GHOSTS + len(FROM_WEST), 128)
     phase, keep, give = call(
         first_kernel, [(4, 16, 128), rows, rows], (fluid, order), [VMEM] * 2, name="moments"
     )
@@ -454,9 +497,9 @@
         (pair,) = call(pair_kernel, [(2, *rows)], (keep, got), [VMEM] * 2, name="pair")
         crossed = cross_planes(pair, steps[step])
         other = swap("gz", crossed, 0)
-        stack, edge = call(
+        stack, edge, one, two = call(
             stack_kernel,
-            [(4, 32, 128), (ITEMS - 3, 8, 128)],
+            [(4, 24, 128), (ITEMS - 3, 8, 128), (56, 128), (56, 128)],
             (phase, crossed, other),
             [VMEM] * 3,
             name="stack",
@@ -464,14 +507,14 @@
         wide, one, two = call(
             functools.partial(ghost_kernel, step),
             [(8, 32, 128), (32, 128), (32, 128)],
-            (offsets, weights, stack, swap("gx", stack, 0), swap("gx", stack, 1)),
+            (offsets, weights, stack, swap("gx", one, 0), swap("gx", two, 1)),
             [SMEM] * 2 + [VMEM] * 3,
             [pltpu.VMEM((12, 32, 128), F32)],
             name="ghosts",
         )
-        post, east, west = call(
+        post, edges, east, west = call(
             collide_kernel,
-            [(38, 4, 16, 128), face, face],
+            [(38, 4, 16, 128), (10, 8, 128), face, face],
             (wide, one, two, swap("gz", one, 0), swap("gz", two, 1), edge, fluid, order),
             [VMEM] * 8,
             [
@@ -485,7 +528,7 @@
         moved, one, two = call(
             functools.partial(stream_kernel, step),
             [(38, 4, 16, 128), (16, 128), (16, 128)],
-            (offsets, weights, post, east, swap("gx", east, 0), swap("gx", west, 1)),
+            (offsets, weights, post, edges, swap("gx", east, 0), swap("gx", west, 1)),
             [SMEM] * 2 + [VMEM] * 4,
             [pltpu.VMEM((2, 12, 16, 128), F32)],
             name="stream",

time: 101 us -> 95.2 us (0.943)
  the two profiles are of different devices: /device:TPU:1 before, /device:TPU:25 now
where the time goes in v1:
time: 95.2 us; the launch traced here: 96.9 us
  starting transfers between devices  47.5 us (50%)
  waiting for transfers between devices  36.2 us (38%)
  Pallas kernels  8.13 us (9%)
  local copies, waits for them, and re-layouts  2.75 us (3%)
  between operations  2.08 us (2%)
    ppermute x20, starting transfers between devices, swap(): return lax.ppermute(values, axis, pairs)  40 us
    ppermute x20, waiting for transfers between devices, swap(): return lax.ppermute(values, axis, pairs)  24.9 us
    ppermute x2, waiting for transfers between devices, branch(): return lambda sent: lax.ppermute(sent, axes, pairs)  11.3 us
    pallas_call x13, Pallas kernels, call(): pl.pallas_call(body, out_shape=[jax.ShapeDtypeStruct(shape, F32) for shap...  8.13 us
    ppermute x2, starting transfers between devices, branch(): return lambda sent: lax.ppermute(sent, axes, pairs)  7.55 us
    unnamed x12, local copies, waits for them, and re-layouts  2.16 us
  transfers between devices with their start and end apart: 22, of which 15 were waited for; matrix products, arithmetic and copies ran while one was open for 1% of the time, Pallas kernels for 0%

profile of v1, /device:TPU:25, one launch (start us, length us, event | category | flops | bytes accessed | tf_op | source)
XLA Modules:
  0.0 96.9 jit_solution(12363776544447183396)
XLA Ops:
  0.6 0.0 copy-start
  0.6 1.1 %copy-done = f32[19,4,16,128]{3,2,1,0:T(8,128)S(1)} copy-done((f32[19,4,16,128]{3,2,1,0:T(8,128)S(1)}, f32[19,4,16,128]{3,2,1,0:T(8,128)}, u32[]{:S(2)}) %copy-start) | copy-done | bytes 622616
  1.7 1.1 %copy-done.2 = f32[19,4,16,128]{3,2,1,0:T(8,128)S(1)} copy-done((f32[19,4,16,128]{3,2,1,0:T(8,128)S(1)}, f32[19,4,16,128]{3,2,1,0:T(8,128)}, u32[]{:S(2)}) %copy-start.2) | copy-done | bytes 622616
  2.8 0.1 moments.1
  2.9 0.8 collective-permute-start.32
  3.7 0.0 copy-done.4
  3.7 0.2 add_reduce_fusion
  3.9 0.6 fusion.1
  5.1 0.0 collective-permute-done.32.got_ref
  5.2 10.1 %conditional.2 = (f32[2,17,4,128]{3,2,1,0:T(4,128)}) conditional(s32[]{:T(128)} %bitcast, f32[2,17,4,128]{3,2,1,0:T(4,128)S(1)} %pair.2, f32[2,17,4,128]{3,2,1,0:T(4,128)S(1)} %pair.2, f32[2,17,4,128]{3,2,1,0:T(4,128)S(1)} %pair.2, f32[2,17,4,128]{3,2,1,0:T(4,128)S(1)} %pair.2, ...), branch_computations={%region_0.1_spmd, %region_1.2_spmd, %region_2.3_spmd, %region_3.4_... | conditional | bytes 278576 | solution.py:483
  5.2 7.5 %collective-permute-start.3 = (f32[2,17,4,128]{3,2,1,0:T(4,128)S(1)}, f32[2,17,4,128]{3,2,1,0:T(4,128)}, u32[]{:S(2)}, u32[]{:S(2)}) collective-permute-start(f32[2,17,4,128]{3,2,1,0:T(4,128)S(1)} %param.3), channel_id=1, source_target_pairs={{0,53},{53,0},{2,55},{55,2},{4,57},{57,4},{6,59},{59,6},{8,61},{61... | collective-permute-start | bytes 208904 | tf_op jit(solution)/shard_map/cond/branch_3_fun/ppermute | solution.py:481
  12.7 2.6 %collective-permute-done.3 = f32[2,17,4,128]{3,2,1,0:T(4,128)} collective-permute-done((f32[2,17,4,128]{3,2,1,0:T(4,128)S(1)}, f32[2,17,4,128]{3,2,1,0:T(4,128)}, u32[]{:S(2)}, u32[]{:S(2)}) %collective-permute-start.3) | collective-permute-done | bytes 69664 | tf_op jit(solution)/shard_map/cond/branch_3_fun/ppermute | solution.py:481
  15.3 1.2 %collective-permute-start.33 = (f32[2,17,4,128]{3,2,1,0:T(4,128)}, f32[2,17,4,128]{3,2,1,0:T(4,128)S(1)}, u32[]{:S(2)}, u32[]{:S(2)}) collective-permute-start(f32[2,17,4,128]{3,2,1,0:T(4,128)} %get-tuple-element.142.crossed_ref), channel_id=1, source_target_pairs={{0,1},{1,0},{2,3},{3,2},{4,5},{5,4},{6,7},{7,6},{8,9},{9,8},{10,11... | collective-permute-start | bytes 208904 | tf_op jit(solution)/shard_map/ppermute | solution.py:459
  16.5 1.1 %collective-permute-done.33.other_ref = f32[2,17,4,128]{3,2,1,0:T(4,128)S(1)} collective-permute-done((f32[2,17,4,128]{3,2,1,0:T(4,128)}, f32[2,17,4,128]{3,2,1,0:T(4,128)S(1)}, u32[]{:S(2)}, u32[]{:S(2)}) %collective-permute-start.33) | collective-permute-done | bytes 69664 | tf_op jit(solution)/shard_map/ppermute | solution.py:459
  17.6 0.9 stack.2
  18.5 1.7 %collective-permute-start.34 = (f32[56,128]{1,0:T(8,128)S(1)}, f32[56,128]{1,0:T(8,128)S(1)}, u32[]{:S(2)}, u32[]{:S(2)}) collective-permute-start(f32[56,128]{1,0:T(8,128)S(1)} %get-tuple-element.108), channel_id=1, source_target_pairs={{0,16},{16,0},{32,48},{48,32},{64,80},{80,64},{96,112},{112,96},{1... | collective-permute-start | bytes 86024 | tf_op jit(solution)/shard_map/ppermute | solution.py:459
  20.2 8.7 %collective-permute-start.35 = (f32[56,128]{1,0:T(8,128)S(1)}, f32[56,128]{1,0:T(8,128)S(1)}, u32[]{:S(2)}, u32[]{:S(2)}) collective-permute-start(f32[56,128]{1,0:T(8,128)S(1)} %get-tuple-element.109), channel_id=1, source_target_pairs={{16,32},{32,16},{48,64},{64,48},{80,96},{96,80},{112,128},{128,112... | collective-permute-start | bytes 86024 | tf_op jit(solution)/shard_map/ppermute | solution.py:459
  28.9 0.0 collective-permute-done.34.one_ref
  28.9 1.3 %collective-permute-done.35.two_ref = f32[56,128]{1,0:T(8,128)S(1)} collective-permute-done((f32[56,128]{1,0:T(8,128)S(1)}, f32[56,128]{1,0:T(8,128)S(1)}, u32[]{:S(2)}, u32[]{:S(2)}) %collective-permute-start.35) | collective-permute-done | bytes 28704 | tf_op jit(solution)/shard_map/ppermute | solution.py:459
  30.1 0.7 ghosts.2
  30.9 1.6 %collective-permute-start.36 = (f32[32,128]{1,0:T(8,128)S(1)}, f32[32,128]{1,0:T(8,128)S(1)}, u32[]{:S(2)}, u32[]{:S(2)}) collective-permute-start(f32[32,128]{1,0:T(8,128)S(1)} %get-tuple-element.111.sent_one), channel_id=1, source_target_pairs={{0,1},{1,0},{2,3},{3,2},{4,5},{5,4},{6,7},{7,6},{8,9},{9,8},{10,11... | collective-permute-start | bytes 49160 | tf_op jit(solution)/shard_map/ppermute | solution.py:459
  32.5 0.9 collective-permute-start.37
  33.4 0.0 collective-permute-done.36.got_one
  33.4 2.3 %collective-permute-done.37.got_two = f32[32,128]{1,0:T(8,128)S(1)} collective-permute-done((f32[32,128]{1,0:T(8,128)S(1)}, f32[32,128]{1,0:T(8,128)S(1)}, u32[]{:S(2)}, u32[]{:S(2)}) %collective-permute-start.37) | collective-permute-done | bytes 16416 | tf_op jit(solution)/shard_map/ppermute | solution.py:459
  35.6 0.0 copy-done.1
  35.6 0.6 collide.2
  36.3 0.1 collective-permute-start.38
  36.4 6.0 %collective-permute-start.39 = (f32[200,128]{1,0:T(8,128)S(1)}, f32[200,128]{1,0:T(8,128)S(1)}, u32[]{:S(2)}, u32[]{:S(2)}) collective-permute-start(f32[200,128]{1,0:T(8,128)S(1)} %get-tuple-element.117), channel_id=1, source_target_pairs={{16,32},{32,16},{48,64},{64,48},{80,96},{96,80},{112,128},{128,112... | collective-permute-start | bytes 307208 | tf_op jit(solution)/shard_map/ppermute | solution.py:459
  42.4 0.0 collective-permute-done.38.one_ref
  42.4 5.2 %collective-permute-done.39.two_ref = f32[200,128]{1,0:T(8,128)S(1)} collective-permute-done((f32[200,128]{1,0:T(8,128)S(1)}, f32[200,128]{1,0:T(8,128)S(1)}, u32[]{:S(2)}, u32[]{:S(2)}) %collective-permute-start.39) | collective-permute-done | bytes 102432 | tf_op jit(solution)/shard_map/ppermute | solution.py:459
  47.6 0.8 stream.2
  48.5 0.5 collective-permute-start.40
  49.0 0.7 collective-permute-start.41
  49.7 0.1 collective-permute-done.40.one_ref
  49.8 2.3 %collective-permute-done.41.two_ref = f32[16,128]{1,0:T(8,128)S(1)} collective-permute-done((f32[16,128]{1,0:T(8,128)S(1)}, f32[16,128]{1,0:T(8,128)S(1)}, u32[]{:S(2)}, u32[]{:S(2)}) %collective-permute-start.41) | collective-permute-done | bytes 8224 | tf_op jit(solution)/shard_map/ppermute | solution.py:459
  52.1 0.4 finish.2
  52.5 0.2 collective-permute-start.42
  53.4 0.5 collective-permute-done.42.got_ref
  53.8 8.8 %conditional.3 = (f32[2,17,4,128]{3,2,1,0:T(4,128)}) conditional(s32[]{:T(128)} %bitcast.1, f32[2,17,4,128]{3,2,1,0:T(4,128)S(1)} %pair.3, f32[2,17,4,128]{3,2,1,0:T(4,128)S(1)} %pair.3, f32[2,17,4,128]{3,2,1,0:T(4,128)S(1)} %pair.3, f32[2,17,4,128]{3,2,1,0:T(4,128)S(1)} %pair.3, ...), branch_computations={%region_16.17_spmd, %region_17.18_spmd, %region_18.19_spmd, %regio... | conditional | bytes 278576 | solution.py:483
  53.8 0.0 collective-permute-start.26
  53.9 8.8 %collective-permute-done.26 = f32[2,17,4,128]{3,2,1,0:T(4,128)} collective-permute-done((f32[2,17,4,128]{3,2,1,0:T(4,128)S(1)}, f32[2,17,4,128]{3,2,1,0:T(4,128)}, u32[]{:S(2)}, u32[]{:S(2)}) %collective-permute-start.26) | collective-permute-done | bytes 69664 | tf_op jit(solution)/shard_map/cond/branch_10_fun/ppermute | solution.py:481
  62.6 0.4 collective-permute-start.43
  63.1 1.1 %collective-permute-done.43.other_ref = f32[2,17,4,128]{3,2,1,0:T(4,128)S(1)} collective-permute-done((f32[2,17,4,128]{3,2,1,0:T(4,128)}, f32[2,17,4,128]{3,2,1,0:T(4,128)S(1)}, u32[]{:S(2)}, u32[]{:S(2)}) %collective-permute-start.43) | collective-permute-done | bytes 69664 | tf_op jit(solution)/shard_map/ppermute | solution.py:459
  64.2 0.9 stack.3
  65.1 0.1 collective-permute-start.44
  65.2 8.3 %collective-permute-start.45 = (f32[56,128]{1,0:T(8,128)S(1)}, f32[56,128]{1,0:T(8,128)S(1)}, u32[]{:S(2)}, u32[]{:S(2)}) collective-permute-start(f32[56,128]{1,0:T(8,128)S(1)} %get-tuple-element.126), channel_id=1, source_target_pairs={{16,32},{32,16},{48,64},{64,48},{80,96},{96,80},{112,128},{128,112... | collective-permute-start | bytes 86024 | tf_op jit(solution)/shard_map/ppermute | solution.py:459
  73.5 0.0 collective-permute-done.44.one_ref
  73.5 1.3 %collective-permute-done.45.two_ref = f32[56,128]{1,0:T(8,128)S(1)} collective-permute-done((f32[56,128]{1,0:T(8,128)S(1)}, f32[56,128]{1,0:T(8,128)S(1)}, u32[]{:S(2)}, u32[]{:S(2)}) %collective-permute-start.45) | collective-permute-done | bytes 28704 | tf_op jit(solution)/shard_map/ppermute | solution.py:459
  74.8 0.7 ghosts.3
  75.5 1.1 %collective-permute-start.46 = (f32[32,128]{1,0:T(8,128)S(1)}, f32[32,128]{1,0:T(8,128)S(1)}, u32[]{:S(2)}, u32[]{:S(2)}) collective-permute-start(f32[32,128]{1,0:T(8,128)S(1)} %get-tuple-element.128.sent_one), channel_id=1, source_target_pairs={{0,1},{1,0},{2,3},{3,2},{4,5},{5,4},{6,7},{7,6},{8,9},{9,8},{10,11... | collective-permute-start | bytes 49160 | tf_op jit(solution)/shard_map/ppermute | solution.py:459
  76.6 0.0 collective-permute-start.47
  76.6 0.8 collective-permute-done.46.got_one
  77.4 2.3 %collective-permute-done.47.got_two = f32[32,128]{1,0:T(8,128)S(1)} collective-permute-done((f32[32,128]{1,0:T(8,128)S(1)}, f32[32,128]{1,0:T(8,128)S(1)}, u32[]{:S(2)}, u32[]{:S(2)}) %collective-permute-start.47) | collective-permute-done | bytes 16416 | tf_op jit(solution)/shard_map/ppermute | solution.py:459
  79.8 0.6 collide.3
  80.4 0.1 collective-permute-start.48
  80.5 6.1 %collective-permute-start.49 = (f32[200,128]{1,0:T(8,128)S(1)}, f32[200,128]{1,0:T(8,128)S(1)}, u32[]{:S(2)}, u32[]{:S(2)}) collective-permute-start(f32[200,128]{1,0:T(8,128)S(1)} %get-tuple-element.136), channel_id=1, source_target_pairs={{16,32},{32,16},{48,64},{64,48},{80,96},{96,80},{112,128},{128,112... | collective-permute-start | bytes 307208 | tf_op jit(solution)/shard_map/ppermute | solution.py:459
  86.6 0.0 collective-permute-done.48.one_ref
  86.6 4.4 %collective-permute-done.49.two_ref = f32[200,128]{1,0:T(8,128)S(1)} collective-permute-done((f32[200,128]{1,0:T(8,128)S(1)}, f32[200,128]{1,0:T(8,128)S(1)}, u32[]{:S(2)}, u32[]{:S(2)}) %collective-permute-start.49) | collective-permute-done | bytes 102432 | tf_op jit(solution)/shard_map/ppermute | solution.py:459
  91.0 0.8 stream.3
  91.9 0.5 collective-permute-start.50
  92.4 1.0 %collective-permute-start.51 = (f32[16,128]{1,0:T(8,128)S(1)}, f32[16,128]{1,0:T(8,128)S(1)}, u32[]{:S(2)}, u32[]{:S(2)}) collective-permute-start(f32[16,128]{1,0:T(8,128)S(1)} %get-tuple-element.139), channel_id=1, source_target_pairs={{1,2},{2,1},{3,0},{0,3},{5,6},{6,5},{7,4},{4,7},{9,10},{10,9},{11,... | collective-permute-start | bytes 24584 | tf_op jit(solution)/shard_map/ppermute | solution.py:459
  93.4 0.0 collective-permute-done.50.one_ref
  93.4 2.1 %collective-permute-done.51.two_ref = f32[16,128]{1,0:T(8,128)S(1)} collective-permute-done((f32[16,128]{1,0:T(8,128)S(1)}, f32[16,128]{1,0:T(8,128)S(1)}, u32[]{:S(2)}, u32[]{:S(2)}) %collective-permute-start.51) | collective-permute-done | bytes 8224 | tf_op jit(solution)/shard_map/ppermute | solution.py:459
  95.5 1.4 %finish.3 = (f32[19,4,16,128]{3,2,1,0:T(8,128)}, f32[19,4,16,128]{3,2,1,0:T(8,128)}) custom-call(f32[38,4,16,128]{3,2,1,0:T(8,128)S(1)} %get-tuple-element.137.moved_ref, f32[16,128]{1,0:T(8,128)S(1)} %collective-permute-done.50.one_ref, f32[16,128]{1,0:T(8,128)S(1)} %collective-permute-done.51.two_ref), custom_call_target="tpu_custom_call" | custom-call | tf_op jit(solution)/shard_map/finish/pallas_call | solution.py:65
  (10 shorter events, 0.0 us)
Async XLA Ops:
  0.6 1.1 %copy-start = (f32[19,4,16,128]{3,2,1,0:T(8,128)S(1)}, f32[19,4,16,128]{3,2,1,0:T(8,128)}, u32[]{:S(2)}) copy-start(f32[19,4,16,128]{3,2,1,0:T(8,128)} %f_ref.3) | copy-start | bytes 1867780
  1.7 1.1 %copy-start.2 = (f32[19,4,16,128]{3,2,1,0:T(8,128)S(1)}, f32[19,4,16,128]{3,2,1,0:T(8,128)}, u32[]{:S(2)}) copy-start(f32[19,4,16,128]{3,2,1,0:T(8,128)} %g_ref.3) | copy-start | bytes 1867780
  2.8 0.9 copy-start.4
  2.8 27.4 %copy-start.5 = (f32[4]{0:T(128)S(1)}, f32[4]{0:T(128)}, u32[]{:S(2)}) copy-start(f32[4]{0:T(128)} %weights.7) | copy-start | bytes 52
  2.8 32.8 %copy-start.1 = (f32[19,4,16,128]{3,2,1,0:T(8,128)S(1)}, f32[19,4,16,128]{3,2,1,0:T(8,128)}, u32[]{:S(2)}) copy-start(f32[19,4,16,128]{3,2,1,0:T(8,128)} %f_ref.3) | copy-start | bytes 1867780
  2.8 32.8 %copy-start.3 = (f32[19,4,16,128]{3,2,1,0:T(8,128)S(1)}, f32[19,4,16,128]{3,2,1,0:T(8,128)}, u32[]{:S(2)}) copy-start(f32[19,4,16,128]{3,2,1,0:T(8,128)} %g_ref.3) | copy-start | bytes 1867780
  2.9 2.2 %collective-permute-start.32 = (f32[17,4,128]{2,1,0:T(4,128)S(1)}, f32[17,4,128]{2,1,0:T(4,128)S(1)}, u32[]{:S(2)}, u32[]{:S(2)}) collective-permute-start(f32[17,4,128]{2,1,0:T(4,128)S(1)} %get-tuple-element.106), channel_id=1, source_target_pairs={{0,1},{1,0},{2,3},{3,2},{4,5},{5,4},{6,7},{7,6},{8,9},{9,8},{10,11... | collective-permute-start | bytes 104456 | tf_op jit(solution)/shard_map/ppermute | solution.py:459
  5.2 10.1 %collective-permute-start.3 = (f32[2,17,4,128]{3,2,1,0:T(4,128)S(1)}, f32[2,17,4,128]{3,2,1,0:T(4,128)}, u32[]{:S(2)}, u32[]{:S(2)}) collective-permute-start(f32[2,17,4,128]{3,2,1,0:T(4,128)S(1)} %param.3), channel_id=1, source_target_pairs={{0,53},{53,0},{2,55},{55,2},{4,57},{57,4},{6,59},{59,6},{8,61},{61... | collective-permute-start | bytes 208904 | tf_op jit(solution)/shard_map/cond/branch_3_fun/ppermute | solution.py:481
  15.3 2.3 %collective-permute-start.33 = (f32[2,17,4,128]{3,2,1,0:T(4,128)}, f32[2,17,4,128]{3,2,1,0:T(4,128)S(1)}, u32[]{:S(2)}, u32[]{:S(2)}) collective-permute-start(f32[2,17,4,128]{3,2,1,0:T(4,128)} %get-tuple-element.142.crossed_ref), channel_id=1, source_target_pairs={{0,1},{1,0},{2,3},{3,2},{4,5},{5,4},{6,7},{7,6},{8,9},{9,8},{10,11... | collective-permute-start | bytes 208904 | tf_op jit(solution)/shard_map/ppermute | solution.py:459
  18.5 10.4 %collective-permute-start.34 = (f32[56,128]{1,0:T(8,128)S(1)}, f32[56,128]{1,0:T(8,128)S(1)}, u32[]{:S(2)}, u32[]{:S(2)}) collective-permute-start(f32[56,128]{1,0:T(8,128)S(1)} %get-tuple-element.108), channel_id=1, source_target_pairs={{0,16},{16,0},{32,48},{48,32},{64,80},{80,64},{96,112},{112,96},{1... | collective-permute-start | bytes 86024 | tf_op jit(solution)/shard_map/ppermute | solution.py:459
  20.2 9.9 %collective-permute-start.35 = (f32[56,128]{1,0:T(8,128)S(1)}, f32[56,128]{1,0:T(8,128)S(1)}, u32[]{:S(2)}, u32[]{:S(2)}) collective-permute-start(f32[56,128]{1,0:T(8,128)S(1)} %get-tuple-element.109), channel_id=1, source_target_pairs={{16,32},{32,16},{48,64},{64,48},{80,96},{96,80},{112,128},{128,112... | collective-permute-start | bytes 86024 | tf_op jit(solution)/shard_map/ppermute | solution.py:459
  30.9 2.5 %collective-permute-start.36 = (f32[32,128]{1,0:T(8,128)S(1)}, f32[32,128]{1,0:T(8,128)S(1)}, u32[]{:S(2)}, u32[]{:S(2)}) collective-permute-start(f32[32,128]{1,0:T(8,128)S(1)} %get-tuple-element.111.sent_one), channel_id=1, source_target_pairs={{0,1},{1,0},{2,3},{3,2},{4,5},{5,4},{6,7},{7,6},{8,9},{9,8},{10,11... | collective-permute-start | bytes 49160 | tf_op jit(solution)/shard_map/ppermute | solution.py:459
  32.5 3.2 %collective-permute-start.37 = (f32[32,128]{1,0:T(8,128)S(1)}, f32[32,128]{1,0:T(8,128)S(1)}, u32[]{:S(2)}, u32[]{:S(2)}) collective-permute-start(f32[32,128]{1,0:T(8,128)S(1)} %get-tuple-element.112.sent_two), channel_id=1, source_target_pairs={{1,2},{2,1},{3,0},{0,3},{5,6},{6,5},{7,4},{4,7},{9,10},{10,9},{11,... | collective-permute-start | bytes 49160 | tf_op jit(solution)/shard_map/ppermute | solution.py:459
  36.3 6.1 %collective-permute-start.38 = (f32[200,128]{1,0:T(8,128)S(1)}, f32[200,128]{1,0:T(8,128)S(1)}, u32[]{:S(2)}, u32[]{:S(2)}) collective-permute-start(f32[200,128]{1,0:T(8,128)S(1)} %get-tuple-element.116), channel_id=1, source_target_pairs={{0,16},{16,0},{32,48},{48,32},{64,80},{80,64},{96,112},{112,96},{1... | collective-permute-start | bytes 307208 | tf_op jit(solution)/shard_map/ppermute | solution.py:459
  36.4 11.3 %collective-permute-start.39 = (f32[200,128]{1,0:T(8,128)S(1)}, f32[200,128]{1,0:T(8,128)S(1)}, u32[]{:S(2)}, u32[]{:S(2)}) collective-permute-start(f32[200,128]{1,0:T(8,128)S(1)} %get-tuple-element.117), channel_id=1, source_target_pairs={{16,32},{32,16},{48,64},{64,48},{80,96},{96,80},{112,128},{128,112... | collective-permute-start | bytes 307208 | tf_op jit(solution)/shard_map/ppermute | solution.py:459
  48.5 1.4 %collective-permute-start.40 = (f32[16,128]{1,0:T(8,128)S(1)}, f32[16,128]{1,0:T(8,128)S(1)}, u32[]{:S(2)}, u32[]{:S(2)}) collective-permute-start(f32[16,128]{1,0:T(8,128)S(1)} %get-tuple-element.119), channel_id=1, source_target_pairs={{0,1},{1,0},{2,3},{3,2},{4,5},{5,4},{6,7},{7,6},{8,9},{9,8},{10,11... | collective-permute-start | bytes 24584 | tf_op jit(solution)/shard_map/ppermute | solution.py:459
  49.0 3.1 %collective-permute-start.41 = (f32[16,128]{1,0:T(8,128)S(1)}, f32[16,128]{1,0:T(8,128)S(1)}, u32[]{:S(2)}, u32[]{:S(2)}) collective-permute-start(f32[16,128]{1,0:T(8,128)S(1)} %get-tuple-element.120), channel_id=1, source_target_pairs={{1,2},{2,1},{3,0},{0,3},{5,6},{6,5},{7,4},{4,7},{9,10},{10,9},{11,... | collective-permute-start | bytes 24584 | tf_op jit(solution)/shard_map/ppermute | solution.py:459
  52.5 1.3 %collective-permute-start.42 = (f32[17,4,128]{2,1,0:T(4,128)S(1)}, f32[17,4,128]{2,1,0:T(4,128)S(1)}, u32[]{:S(2)}, u32[]{:S(2)}) collective-permute-start(f32[17,4,128]{2,1,0:T(4,128)S(1)} %get-tuple-element.123), channel_id=1, source_target_pairs={{0,1},{1,0},{2,3},{3,2},{4,5},{5,4},{6,7},{7,6},{8,9},{9,8},{10,11... | collective-permute-start | bytes 104456 | tf_op jit(solution)/shard_map/ppermute | solution.py:459
  53.8 8.8 %collective-permute-start.26 = (f32[2,17,4,128]{3,2,1,0:T(4,128)S(1)}, f32[2,17,4,128]{3,2,1,0:T(4,128)}, u32[]{:S(2)}, u32[]{:S(2)}) collective-permute-start(f32[2,17,4,128]{3,2,1,0:T(4,128)S(1)} %param.26), channel_id=1, source_target_pairs={{0,165},{165,0},{2,167},{167,2},{4,169},{169,4},{6,171},{171,6},{8... | collective-permute-start | bytes 208904 | tf_op jit(solution)/shard_map/cond/branch_10_fun/ppermute | solution.py:481
  62.6 1.6 %collective-permute-start.43 = (f32[2,17,4,128]{3,2,1,0:T(4,128)}, f32[2,17,4,128]{3,2,1,0:T(4,128)S(1)}, u32[]{:S(2)}, u32[]{:S(2)}) collective-permute-start(f32[2,17,4,128]{3,2,1,0:T(4,128)} %get-tuple-element.143.crossed_ref), channel_id=1, source_target_pairs={{0,1},{1,0},{2,3},{3,2},{4,5},{5,4},{6,7},{7,6},{8,9},{9,8},{10,11... | collective-permute-start | bytes 208904 | tf_op jit(solution)/shard_map/ppermute | solution.py:459
  65.1 8.4 %collective-permute-start.44 = (f32[56,128]{1,0:T(8,128)S(1)}, f32[56,128]{1,0:T(8,128)S(1)}, u32[]{:S(2)}, u32[]{:S(2)}) collective-permute-start(f32[56,128]{1,0:T(8,128)S(1)} %get-tuple-element.125), channel_id=1, source_target_pairs={{0,16},{16,0},{32,48},{48,32},{64,80},{80,64},{96,112},{112,96},{1... | collective-permute-start | bytes 86024 | tf_op jit(solution)/shard_map/ppermute | solution.py:459
  65.2 9.5 %collective-permute-start.45 = (f32[56,128]{1,0:T(8,128)S(1)}, f32[56,128]{1,0:T(8,128)S(1)}, u32[]{:S(2)}, u32[]{:S(2)}) collective-permute-start(f32[56,128]{1,0:T(8,128)S(1)} %get-tuple-element.126), channel_id=1, source_target_pairs={{16,32},{32,16},{48,64},{64,48},{80,96},{96,80},{112,128},{128,112... | collective-permute-start | bytes 86024 | tf_op jit(solution)/shard_map/ppermute | solution.py:459
  75.5 2.0 %collective-permute-start.46 = (f32[32,128]{1,0:T(8,128)S(1)}, f32[32,128]{1,0:T(8,128)S(1)}, u32[]{:S(2)}, u32[]{:S(2)}) collective-permute-start(f32[32,128]{1,0:T(8,128)S(1)} %get-tuple-element.128.sent_one), channel_id=1, source_target_pairs={{0,1},{1,0},{2,3},{3,2},{4,5},{5,4},{6,7},{7,6},{8,9},{9,8},{10,11... | collective-permute-start | bytes 49160 | tf_op jit(solution)/shard_map/ppermute | solution.py:459
  76.6 3.2 %collective-permute-start.47 = (f32[32,128]{1,0:T(8,128)S(1)}, f32[32,128]{1,0:T(8,128)S(1)}, u32[]{:S(2)}, u32[]{:S(2)}) collective-permute-start(f32[32,128]{1,0:T(8,128)S(1)} %get-tuple-element.129.sent_two), channel_id=1, source_target_pairs={{1,2},{2,1},{3,0},{0,3},{5,6},{6,5},{7,4},{4,7},{9,10},{10,9},{11,... | collective-permute-start | bytes 49160 | tf_op jit(solution)/shard_map/ppermute | solution.py:459
  80.4 6.2 %collective-permute-start.48 = (f32[200,128]{1,0:T(8,128)S(1)}, f32[200,128]{1,0:T(8,128)S(1)}, u32[]{:S(2)}, u32[]{:S(2)}) collective-permute-start(f32[200,128]{1,0:T(8,128)S(1)} %get-tuple-element.135), channel_id=1, source_target_pairs={{0,16},{16,0},{32,48},{48,32},{64,80},{80,64},{96,112},{112,96},{1... | collective-permute-start | bytes 307208 | tf_op jit(solution)/shard_map/ppermute | solution.py:459
  80.5 10.5 %collective-permute-start.49 = (f32[200,128]{1,0:T(8,128)S(1)}, f32[200,128]{1,0:T(8,128)S(1)}, u32[]{:S(2)}, u32[]{:S(2)}) collective-permute-start(f32[200,128]{1,0:T(8,128)S(1)} %get-tuple-element.136), channel_id=1, source_target_pairs={{16,32},{32,16},{48,64},{64,48},{80,96},{96,80},{112,128},{128,112... | collective-permute-start | bytes 307208 | tf_op jit(solution)/shard_map/ppermute | solution.py:459
  91.9 1.5 %collective-permute-start.50 = (f32[16,128]{1,0:T(8,128)S(1)}, f32[16,128]{1,0:T(8,128)S(1)}, u32[]{:S(2)}, u32[]{:S(2)}) collective-permute-start(f32[16,128]{1,0:T(8,128)S(1)} %get-tuple-element.138), channel_id=1, source_target_pairs={{0,1},{1,0},{2,3},{3,2},{4,5},{5,4},{6,7},{7,6},{8,9},{9,8},{10,11... | collective-permute-start | bytes 24584 | tf_op jit(solution)/shard_map/ppermute | solution.py:459
  92.4 3.1 %collective-permute-start.51 = (f32[16,128]{1,0:T(8,128)S(1)}, f32[16,128]{1,0:T(8,128)S(1)}, u32[]{:S(2)}, u32[]{:S(2)}) collective-permute-start(f32[16,128]{1,0:T(8,128)S(1)} %get-tuple-element.139), channel_id=1, source_target_pairs={{1,2},{2,1},{3,0},{0,3},{5,6},{6,5},{7,4},{4,7},{9,10},{10,9},{11,... | collective-permute-start | bytes 24584 | tf_op jit(solution)/shard_map/ppermute | solution.py:459

commit v2 on v1

--- a/solution.py
+++ b/solution.py
@@ -51,9 +51,13 @@
 ITEMS = 17
 
 REACH = [(k, side, (1 - 2 * side) * VELOCITIES[RISING[k % 5]][0]) for k in range(10) for side in (0, 1)]
+REACH += [(10, 0, 0), (10, 1, 0)]
 FROM_WEST = [(k, side, place) for k, side, cx in REACH for place in range(2 - cx, 4)]
 FROM_EAST = [(k, side, place) for k, side, cx in REACH for place in range(8, 10 - cx)]
-GHOSTS = 160
+CORNERS = 160
+GHOSTS = 176
+FACE_ROWS = 224
+SIDES = ((5, FRONT), (4, BACK))
 FAR = (1, 2, 8, 9, 22, 23, 28, 29)
 
 VMEM = pl.BlockSpec(memory_space=pltpu.VMEM)
@@ -103,8 +107,11 @@
     return jnp.where(odd, two, one), jnp.where(odd, one, two)
 
 
-def edge_messages(fluid, order, phase_ref, keep_ref, give_ref):
+def edge_messages(fluid, order, phase_ref, keep_ref, give_ref, first_ref, last_ref):
     odd = is_odd("gz")
+    lane = lanes((16, 128))
+    first = jnp.zeros((16, 128), F32)
+    last = jnp.zeros((16, 128), F32)
 
     def put(item, x, low, high):
         keep, give = swapped(odd, high, low)
@@ -118,16 +125,30 @@
         phase_ref[x] = phase
         for item in range(3):
             put(item, x, phase[item : item + 1], phase[13 + item : 14 + item])
-        fields = [sum(f[1:], f[0])]
-        for q in range(3):
-            plus = [f[i] for i, c in enumerate(VELOCITIES) if c[q] == 1]
-            minus = [f[i] for i, c in enumerate(VELOCITIES) if c[q] == -1]
-            fields.append(sum(plus[1:], plus[0]) - sum(minus[1:], minus[0]))
+        density, momentum = moments(f)
+        fields = [density, *momentum]
         for n, field in enumerate(fields):
             put(3 + n, x, field[0:1], field[15:16])
         for n in range(5):
             put(7 + n, x, f[FALLING[n]][0:1], f[RISING[n]][15:16])
             put(12 + n, x, g[FALLING[n]][0:1], g[RISING[n]][15:16])
+        front = [f[i] for i in FRONT] + [g[i] for i in FRONT] + fields
+        back = [f[i] for i in BACK] + [g[i] for i in BACK] + fields
+        for n in range(14):
+            at = 8 * n + 2 * x
+            last = jnp.where(lane == at, shift(front[n], at - 127, 1), last)
+            first = jnp.where(lane == at, shift(back[n], at, 1), first)
+    first_ref[...] = first
+    last_ref[...] = last
+
+
+def moments(f):
+    momentum = []
+    for q in range(3):
+        plus = [f[i] for i, c in enumerate(VELOCITIES) if c[q] == 1]
+        minus = [f[i] for i, c in enumerate(VELOCITIES) if c[q] == -1]
+        momentum.append(sum(plus[1:], plus[0]) - sum(minus[1:], minus[0]))
+    return sum(f[1:], f[0]), momentum
 
 
 def first_kernel(f_ref, g_ref, *rest):
@@ -166,7 +187,19 @@
 
 
 def ghost_kernel(
-    step, offsets, weights, own_ref, one_ref, two_ref, phase_ref, send_one, send_two, wide
+    step,
+    offsets,
+    weights,
+    own_ref,
+    one_ref,
+    two_ref,
+    edge_ref,
+    first_ref,
+    last_ref,
+    phase_ref,
+    send_one,
+    send_two,
+    wide,
 ):
     up, down = planes()
     r_down = plane_shift(offsets, step, down)
@@ -214,8 +247,28 @@
             value = jnp.where((row == 26) | (row == 27), shift(rise(place, r_up, w_up), 4, 0), value)
         phase_ref[n] = value
         first = jnp.where(lane // 2 == n, shift(value, 2 * n, 1), first)
+        first = jnp.where(lane == 32 + 2 * n, shift(value, 30 + 2 * n, 1), first)
         last = jnp.where(lane // 2 == n, shift(value, 2 * n - 126, 1), last)
-    send_one[...], send_two[...] = swapped(is_odd("gz"), last, first)
+        last = jnp.where(lane == 33 + 2 * n, shift(value, 2 * n - 92, 1), last)
+
+    shape = (8, 128)
+    lane = lanes(shape)
+    below = rows_of(shape) < 4
+    edge_first = jnp.zeros(shape, F32)
+    edge_last = jnp.zeros(shape, F32)
+    for n in range(6):
+        if n < 4:
+            front = back = edge_ref[n]
+        else:
+            one, two = edge_ref[5 * n - 13], edge_ref[5 * n - 12]
+            front, back = jnp.where(below, one, two), jnp.where(below, two, one)
+        edge_last = jnp.where(lane == n, shift(front, n - 127, 1), edge_last)
+        edge_first = jnp.where(lane == n, shift(back, n, 1), edge_first)
+
+    odd = is_odd("gz")
+    send_one[0:32, :], send_two[0:32, :] = swapped(odd, last, first)
+    send_one[32:48, :], send_two[32:48, :] = swapped(odd, last_ref[...], first_ref[...])
+    send_one[48:56, :], send_two[48:56, :] = swapped(odd, edge_last, edge_first)
 
 
 def bulk_potential(phase, around):
@@ -232,6 +285,7 @@
     f_ref,
     g_ref,
     post_ref,
+    columns_ref,
     edges_ref,
     send_one,
     send_two,
@@ -243,8 +297,10 @@
     shape = (32, 128)
     lane = lanes(shape)
     odd = is_odd("gz")
-    last, first = swapped(odd, sent_one[...], sent_two[...])
-    right, left = swapped(odd, got_one[...], got_two[...])
+    last, first = swapped(odd, sent_one[0:32, :], sent_two[0:32, :])
+    right, left = swapped(odd, got_one[0:32, :], got_two[0:32, :])
+    raw_right, raw_left = swapped(odd, got_one[32:48, :], got_two[32:48, :])
+    edge_right, edge_left = swapped(odd, got_one[48:56, :], got_two[48:56, :])
 
     def updown(value):
         return shift(value, 1, 0) + shift(value, -1, 0)
@@ -256,12 +312,25 @@
         right,
         shift(right, 2, 1) + shift(right, -2, 1) + updown(right) + shift(right, -1, 1) + shift(last, -1, 1),
     )
+    outer = shift(left, 1, 1)
+    outer_left = bulk_potential(
+        outer, shift(outer, 2, 1) + shift(outer, -2, 1) + updown(outer) + left + shift(left, -32, 1)
+    )
+    outer = shift(right, -1, 1)
+    outer_right = bulk_potential(
+        outer, shift(outer, 2, 1) + shift(outer, -2, 1) + updown(outer) + right + shift(right, -32, 1)
+    )
+    inner_left = jnp.zeros(shape, F32)
+    inner_right = jnp.zeros(shape, F32)
     for n in range(1, 7):
         value = phase_ref[n]
         before = jnp.where(lane == 0, shift(left, -(2 * n + 1), 1), shift(value, 1, 1))
         after = jnp.where(lane == 127, shift(right, 127 - 2 * n, 1), shift(value, -1, 1))
         around = phase_ref[n - 1] + phase_ref[n + 1] + updown(value) + before + after
-        pots[n] = bulk_potential(value, around)
+        pot = bulk_potential(value, around)
+        pots[n] = pot
+        inner_left = jnp.where(lane == 2 * n + 1, shift(pot, 2 * n + 1, 1), inner_left)
+        inner_right = jnp.where(lane == 2 * n, shift(pot, 2 * n - 127, 1), inner_right)
 
     for x in range(4):
         n = x + 2
@@ -281,12 +350,7 @@
         grad = (gx_all[own], gy_all[own], gz_all[own])
 
         f = [f_ref[i, x] for i in range(19)]
-        density = sum(f[1:], f[0])
-        momentum = []
-        for q in range(3):
-            plus = [f[i] for i, c in enumerate(VELOCITIES) if c[q] == 1]
-            minus = [f[i] for i, c in enumerate(VELOCITIES) if c[q] == -1]
-            momentum.append(sum(plus[1:], plus[0]) - sum(minus[1:], minus[0]))
+        density, momentum = moments(f)
         inverse = 1.0 / density
         speed = [m * inverse for m in momentum]
         force = TAU_F * phase * inverse
@@ -326,28 +390,58 @@
             store(i + 1, keep_f * f[i + 1] + (even - odd), keep_g * g_ref[i + 1, x] + (g_even - g_odd))
 
     sign = jnp.where(rows_of((8, 128)) < 4, 1.0, -1.0)
-    phase, pot, gx, gy, gz = (ghost[k] for k in range(5))
-    density = edge_ref[0]
-    inverse = 1.0 / density
-    speed = [edge_ref[1 + q] * inverse for q in range(3)]
-    force = TAU_F * phase * inverse
-    shifted = [s - force * d for s, d in zip(speed, (gx, gy, gz))]
-    square = shifted[0] * shifted[0] + shifted[1] * shifted[1] + shifted[2] * shifted[2]
-    rest = 1.0 - 1.5 * square
+    flow = Flow(edge_ref[0], [edge_ref[1 + q] for q in range(3)], *(ghost[k] for k in range(5)))
     for k, i in enumerate(RISING):
-        along = sign * directed(VELOCITIES[i], shifted)
-        flow = sign * directed(VELOCITIES[i], speed)
-        feq = WEIGHTS[i] * density * (rest + 3.0 * along + 4.5 * along * along)
-        fs = (1.0 - 1.0 / TAU_F) * edge_ref[4 + k] + (1.0 / TAU_F) * feq
-        fs = fs - (3.0 * WEIGHTS[i] * VELOCITIES[i][0] * U) * density
-        geq = WEIGHTS[i] * (3.0 * M * pot + 3.0 * phase * flow)
-        gs = (1.0 - 1.0 / TAU_G) * edge_ref[9 + k] + (1.0 / TAU_G) * geq
-        edges_ref[k] = fs
+        fs, gs = flow.relax(i, edge_ref[4 + k], edge_ref[9 + k], sign)
+        edges_ref[k] = fs - (3.0 * WEIGHTS[i] * VELOCITIES[i][0] * U) * flow.density
         edges_ref[5 + k] = gs
+
+    small = lanes((8, 128))
+    corner = lanes((16, 128))
+    corner_east = jnp.zeros((16, 128), F32)
+    corner_west = jnp.zeros((16, 128), F32)
+    edge_columns = jnp.zeros((8, 128), F32)
+    around = ((left, left_pot, outer_left, inner_left), (right, right_pot, inner_right, outer_right))
+    for side, (lane0, components) in enumerate(SIDES):
+        phase, pot, before, after = around[side]
+        gx = 0.5 * (shift(pot, -2, 1) - shift(pot, 2, 1))
+        gy = 0.5 * (shift(pot, -1, 0) - shift(pot, 1, 0))
+        gz = 0.5 * (after - before)
+        fields = (phase, pot, gx, gy, gz)
+        raw = (raw_left, raw_right)[side]
+        raw = [shift(raw, lane0 - 8 * n, 1) for n in range(14)]
+        flow = Flow(raw[10], raw[11:], *(value[OWN : OWN + 16] for value in fields))
+        for k, i in enumerate(components):
+            for part, value in enumerate(flow.relax(i, raw[k], raw[5 + k])):
+                columns_ref[10 * side + 5 * part + k] = value
+                at = 2 * side + part
+                if VELOCITIES[i][0] == 1:
+                    corner_east = jnp.where(corner == at, shift(value, at - 6 - lane0, 1), corner_east)
+                elif VELOCITIES[i][0] == -1:
+                    corner_west = jnp.where(corner == at, shift(value, at - lane0, 1), corner_west)
+        for k, value in enumerate(fields):
+            for x in range(4):
+                at = -(2 * x + lane0)
+                ghost[k, x : x + 1, :] = shift(value[0:8], at, 1)[BELOW_EDGE : BELOW_EDGE + 1]
+                high = ABOVE_EDGE - 24
+                ghost[k, 4 + x : 5 + x, :] = shift(value[24:32], at, 1)[high : high + 1]
+        edge = (edge_left, edge_right)[side]
+        edge = [shift(edge, -n, 1) for n in range(6)]
+        flow = Flow(edge[0], edge[1:4], *(ghost[k] for k in range(5)))
+        turn = (sign, 1.0 - 2.0 * side)
+        for part, value in enumerate(flow.relax(15, edge[4], edge[5], turn=turn)):
+            at = 2 * side + part
+            edge_columns = jnp.where(small == at, shift(value, at, 1), edge_columns)
+    edges_ref[10] = edge_columns
+
     odd = is_odd("gx")
     for k in range(10):
         rows = slice(16 * k, 16 * k + 16)
         send_one[rows, :], send_two[rows, :] = swapped(odd, east[k], west[k])
+    rows = slice(CORNERS, CORNERS + 16)
+    send_one[rows, :], send_two[rows, :] = swapped(odd, corner_east, corner_west)
+    for ref in (send_one, send_two):
+        ref[FACE_ROWS - 8 : FACE_ROWS, :] = jnp.zeros((8, 128), F32)
     for n, (to_east, to_west) in enumerate(zip(FROM_WEST, FROM_EAST)):
         values = []
         for k, side, place in (to_east, to_west):
@@ -355,6 +449,33 @@
             values.append(edges_ref[k, at : at + 1, :])
         at = slice(GHOSTS + n, GHOSTS + n + 1)
         send_one[at, :], send_two[at, :] = swapped(odd, *values)
+
+
+class Flow:
+    def __init__(self, density, momentum, phase, pot, gx, gy, gz):
+        inverse = 1.0 / density
+        self.density = density
+        self.phase = phase
+        self.pot = pot
+        self.speed = [m * inverse for m in momentum]
+        force = TAU_F * phase * inverse
+        self.shifted = [s - force * d for s, d in zip(self.speed, (gx, gy, gz))]
+        square = sum(part * part for part in self.shifted)
+        self.rest = 1.0 - 1.5 * square
+
+    def relax(self, i, f, g, sign=None, turn=None):
+        if turn is not None:
+            along, flow = (turn[0] * v[1] + turn[1] * v[2] for v in (self.shifted, self.speed))
+        else:
+            along, flow = (directed(VELOCITIES[i], v) for v in (self.shifted, self.speed))
+        if sign is not None:
+            along, flow = sign * along, sign * flow
+        feq = WEIGHTS[i] * self.density * (self.rest + 3.0 * along + 4.5 * along * along)
+        geq = WEIGHTS[i] * (3.0 * M * self.pot + 3.0 * self.phase * flow)
+        return (
+            (1.0 - 1.0 / TAU_F) * f + (1.0 / TAU_F) * feq,
+            (1.0 - 1.0 / TAU_G) * g + (1.0 / TAU_G) * geq,
+        )
 
 
 def directed(velocity, parts):
@@ -368,15 +489,16 @@
 
 
 def stream_kernel(
-    step, offsets, weights, post_ref, own_ref, one_ref, two_ref, out_ref, send_one, send_two, wide
+    step, more, offsets, weights, post_ref, columns_ref, own_ref, one_ref, two_ref, f_ref, g_ref, *rest
 ):
+    *rest, wide, columns = rest
     up, down = planes()
     r_down = plane_shift(offsets, step, down)
     r_up = plane_shift(offsets, step, up)
     w_down = weights[down]
     w_up = weights[up]
     odd = is_odd("gx")
-    for k in range(10):
+    for k in range(11):
         for side in (0, 1):
             for x in range(4):
                 at = 4 * side + x
@@ -390,17 +512,41 @@
     shape = (16, 128)
     row = rows_of(shape)
     lane = lanes(shape)
-    first = jnp.zeros(shape, F32)
-    last = jnp.zeros(shape, F32)
+
+    def rise(x, c):
+        at = x + 4 - c - r_down
+        return w_down * wide[0, at] + (1.0 - w_down) * wide[0, at - 1]
+
+    def fall(x, c):
+        at = x + 4 - c + r_up
+        return w_up * wide[1, at] + (1.0 - w_up) * wide[1, at + 1]
+
+    rows = slice(CORNERS, CORNERS + 16)
+    corner_east, corner_west = swapped(odd, one_ref[rows, :], two_ref[rows, :])
+    risen = [rise(x, 0)[10:11] for x in range(4)]
+    fallen = [fall(x, 0)[10:11] for x in range(4)]
+    for side, (lane0, components) in enumerate(SIDES):
+        for part in (0, 1):
+            source = 2 * side + part
+            for k, i in enumerate(components):
+                cx, cy, _ = VELOCITIES[i]
+                value = columns_ref[10 * side + 5 * part + k]
+                if cx:
+                    at = lane0 if cx == 1 else lane0 + 6
+                    corner = corner_west if cx == 1 else corner_east
+                    value = jnp.where(lane == at, shift(corner, at - source, 1), shift(value, 2 * cx, 1))
+                if cy:
+                    value = shift(value, cy, 0)
+                    edge = 0 if cy == 1 else 15
+                    for x in range(4):
+                        at = lane0 + 2 * x
+                        ghost = shift((risen if cy == 1 else fallen)[x], at - source, 1)
+                        value = jnp.where((row == edge) & (lane == at), ghost, value)
+                columns[10 * side + 5 * part + k] = value
+
     for x in range(4):
-        place = x + 4
-        risen = {}
-        fallen = {}
-        for c in (-1, 0, 1):
-            at = place - c - r_down
-            risen[c] = w_down * wide[0, at] + (1.0 - w_down) * wide[0, at - 1]
-            at = place - c + r_up
-            fallen[c] = w_up * wide[1, at] + (1.0 - w_up) * wide[1, at + 1]
+        risen = {c: rise(x, c) for c in (-1, 0, 1)}
+        fallen = {c: fall(x, c) for c in (-1, 0, 1)}
         for i in range(38):
             part, component = divmod(i, 19)
             cx, cy, cz = VELOCITIES[component]
@@ -421,30 +567,12 @@
             elif cy == -1:
                 k = 5 * part + FALLING.index(component)
                 value = jnp.where(row == 15, fallen[cx][k : k + 1], shift(value, -1, 0))
-            out_ref[i, x] = value
             if cz == 1:
-                at = 4 * (5 * part + FRONT.index(component)) + x
-                last = jnp.where(lane == at, shift(value, at - 127, 1), last)
+                column = columns[5 * part + FRONT.index(component)]
+                value = jnp.where(lane == 0, shift(column, -(2 * x + 5), 1), shift(value, 1, 1))
             elif cz == -1:
-                at = 4 * (5 * part + BACK.index(component)) + x
-                first = jnp.where(lane == at, shift(value, at, 1), first)
-    send_one[...], send_two[...] = swapped(is_odd("gz"), last, first)
-
-
-def finish_kernel(more, moved_ref, one_ref, two_ref, f_ref, g_ref, *rest):
-    lane = lanes((16, 128))
-    right, left = swapped(is_odd("gz"), one_ref[...], two_ref[...])
-    for x in range(4):
-        for i in range(38):
-            part, component = divmod(i, 19)
-            value = moved_ref[i, x]
-            cz = VELOCITIES[component][2]
-            if cz == 1:
-                at = 4 * (5 * part + FRONT.index(component)) + x
-                value = jnp.where(lane == 0, shift(left, -at, 1), shift(value, 1, 1))
-            elif cz == -1:
-                at = 4 * (5 * part + BACK.index(component)) + x
-                value = jnp.where(lane == 127, shift(right, 127 - at, 1), shift(value, -1, 1))
+                column = columns[10 + 5 * part + BACK.index(component)]
+                value = jnp.where(lane == 127, shift(column, 127 - (2 * x + 4), 1), shift(value, -1, 1))
             (g_ref if part else f_ref)[component, x] = value
     if more:
         edge_messages(lambda i, x: f_ref[i, x], lambda i, x: g_ref[i, x], *rest)
@@ -488,9 +616,10 @@
     steps = (offsets[:, plane] + 2) // 4 % 16
     state = (19, 4, 16, 128)
     rows = (ITEMS, 4, 128)
-    face = (GHOSTS + len(FROM_WEST), 128)
-    phase, keep, give = call(
-        first_kernel, [(4, 16, 128), rows, rows], (fluid, order), [VMEM] * 2, name="moments"
+    face = (FACE_ROWS, 128)
+    before = [(4, 16, 128), rows, rows, (16, 128), (16, 128)]
+    phase, keep, give, first, last = call(
+        first_kernel, before, (fluid, order), [VMEM] * 2, name="moments"
     )
     for step in range(STEPS):
         got = swap("gz", give, 0)
@@ -506,15 +635,15 @@
         )
         wide, one, two = call(
             functools.partial(ghost_kernel, step),
-            [(8, 32, 128), (32, 128), (32, 128)],
-            (offsets, weights, stack, swap("gx", one, 0), swap("gx", two, 1)),
-            [SMEM] * 2 + [VMEM] * 3,
+            [(8, 32, 128), (56, 128), (56, 128)],
+            (offsets, weights, stack, swap("gx", one, 0), swap("gx", two, 1), edge, first, last),
+            [SMEM] * 2 + [VMEM] * 6,
             [pltpu.VMEM((12, 32, 128), F32)],
             name="ghosts",
         )
-        post, edges, east, west = call(
+        post, columns, edges, east, west = call(
             collide_kernel,
-            [(38, 4, 16, 128), (10, 8, 128), face, face],
+            [(38, 4, 16, 128), (20, 16, 128), (11, 8, 128), face, face],
             (wide, one, two, swap("gz", one, 0), swap("gz", two, 1), edge, fluid, order),
             [VMEM] * 8,
             [
@@ -525,25 +654,18 @@
             ],
             name="collide",
         )
-        moved, one, two = call(
-            functools.partial(stream_kernel, step),
-            [(38, 4, 16, 128), (16, 128), (16, 128)],
-            (offsets, weights, post, edges, swap("gx", east, 0), swap("gx", west, 1)),
-            [SMEM] * 2 + [VMEM] * 4,
-            [pltpu.VMEM((2, 12, 16, 128), F32)],
-            name="stream",
-        )
         more = step + 1 < STEPS
         outs = call(
-            functools.partial(finish_kernel, more),
-            [state, state] + ([(4, 16, 128), rows, rows] if more else []),
-            (moved, swap("gz", one, 0), swap("gz", two, 1)),
-            [VMEM] * 3,
-            name="finish",
+            functools.partial(stream_kernel, step, more),
+            [state, state] + (before if more else []),
+            (offsets, weights, post, columns, edges, swap("gx", east, 0), swap("gx", west, 1)),
+            [SMEM] * 2 + [VMEM] * 5,
+            [pltpu.VMEM((2, 12, 16, 128), F32), pltpu.VMEM((20, 16, 128), F32)],
+            name="stream",
         )
         fluid, order = outs[:2]
         if more:
-            phase, keep, give = outs[2:]
+            phase, keep, give, first, last = outs[2:]
     return (fluid, order)
 
 

time: 95.2 us -> 93.5 us (0.982)
  the two profiles are of different devices: /device:TPU:25 before, /device:TPU:1 now
where the time goes in v2:
time: 93.5 us; the launch traced here: 93.6 us
  starting transfers between devices  43.9 us (47%)
  waiting for transfers between devices  35.2 us (38%)
  Pallas kernels  9.52 us (10%)
  local copies, waits for them, and re-layouts  2.75 us (3%)
  between operations  2.06 us (2%)
    ppermute x16, starting transfers between devices, swap(): return lax.ppermute(values, axis, pairs)  34.7 us
    ppermute x16, waiting for transfers between devices, swap(): return lax.ppermute(values, axis, pairs)  29.5 us
    pallas_call x11, Pallas kernels, call(): pl.pallas_call(body, out_shape=[jax.ShapeDtypeStruct(shape, F32) for shap...  9.52 us
    ppermute x2, starting transfers between devices, branch(): return lambda sent: lax.ppermute(sent, axes, pairs)  9.18 us
    ppermute x2, waiting for transfers between devices, branch(): return lambda sent: lax.ppermute(sent, axes, pairs)  5.74 us
    unnamed x12, local copies, waits for them, and re-layouts  2.16 us
  transfers between devices with their start and end apart: 18, of which 14 were waited for; matrix products, arithmetic and copies ran while one was open for 1% of the time, Pallas kernels for 0%

profile of v2, /device:TPU:1, one launch (start us, length us, event | category | flops | bytes accessed | tf_op | source)
XLA Modules:
  0.0 93.6 jit_solution(7808222535327855406)
XLA Ops:
  0.6 0.0 copy-start
  0.6 1.1 %copy-done = f32[19,4,16,128]{3,2,1,0:T(8,128)S(1)} copy-done((f32[19,4,16,128]{3,2,1,0:T(8,128)S(1)}, f32[19,4,16,128]{3,2,1,0:T(8,128)}, u32[]{:S(2)}) %copy-start) | copy-done | bytes 622616
  1.7 0.0 copy-start.2
  1.7 1.1 %copy-done.2 = f32[19,4,16,128]{3,2,1,0:T(8,128)S(1)} copy-done((f32[19,4,16,128]{3,2,1,0:T(8,128)S(1)}, f32[19,4,16,128]{3,2,1,0:T(8,128)}, u32[]{:S(2)}) %copy-start.2) | copy-done | bytes 622616
  2.8 0.0 copy-start.4
  2.8 0.0 copy-start.5
  2.8 0.0 copy-start.1
  2.8 0.0 copy-start.3
  2.8 0.3 moments.1
  3.1 3.3 %collective-permute-start.32 = (f32[17,4,128]{2,1,0:T(4,128)S(1)}, f32[17,4,128]{2,1,0:T(4,128)S(1)}, u32[]{:S(2)}, u32[]{:S(2)}) collective-permute-start(f32[17,4,128]{2,1,0:T(4,128)S(1)} %get-tuple-element.106), channel_id=1, source_target_pairs={{0,1},{1,0},{2,3},{3,2},{4,5},{5,4},{6,7},{7,6},{8,9},{9,8},{10,11... | collective-permute-start | bytes 104456 | tf_op jit(solution)/shard_map/ppermute | solution.py:587
  6.4 0.0 copy-done.4
  6.4 0.2 add_reduce_fusion
  6.6 0.6 fusion.1
  7.9 0.0 collective-permute-done.32.got_ref
  7.9 9.8 %conditional.2 = (f32[2,17,4,128]{3,2,1,0:T(4,128)}) conditional(s32[]{:T(128)} %bitcast, f32[2,17,4,128]{3,2,1,0:T(4,128)S(1)} %pair.2, f32[2,17,4,128]{3,2,1,0:T(4,128)S(1)} %pair.2, f32[2,17,4,128]{3,2,1,0:T(4,128)S(1)} %pair.2, f32[2,17,4,128]{3,2,1,0:T(4,128)S(1)} %pair.2, ...), branch_computations={%region_0.1_spmd, %region_1.2_spmd, %region_2.3_spmd, %region_3.4_... | conditional | bytes 278576 | solution.py:611
  7.9 6.1 %collective-permute-start.9 = (f32[2,17,4,128]{3,2,1,0:T(4,128)S(1)}, f32[2,17,4,128]{3,2,1,0:T(4,128)}, u32[]{:S(2)}, u32[]{:S(2)}) collective-permute-start(f32[2,17,4,128]{3,2,1,0:T(4,128)S(1)} %param.9), channel_id=1, source_target_pairs={{0,149},{149,0},{2,151},{151,2},{4,153},{153,4},{6,155},{155,6},{8... | collective-permute-start | bytes 208904 | tf_op jit(solution)/shard_map/cond/branch_9_fun/ppermute | solution.py:609
  14.1 3.6 %collective-permute-done.9 = f32[2,17,4,128]{3,2,1,0:T(4,128)} collective-permute-done((f32[2,17,4,128]{3,2,1,0:T(4,128)S(1)}, f32[2,17,4,128]{3,2,1,0:T(4,128)}, u32[]{:S(2)}, u32[]{:S(2)}) %collective-permute-start.9) | collective-permute-done | bytes 69664 | tf_op jit(solution)/shard_map/cond/branch_9_fun/ppermute | solution.py:609
  17.7 0.0 collective-permute-start.33
  17.7 1.5 %collective-permute-done.33.other_ref = f32[2,17,4,128]{3,2,1,0:T(4,128)S(1)} collective-permute-done((f32[2,17,4,128]{3,2,1,0:T(4,128)}, f32[2,17,4,128]{3,2,1,0:T(4,128)S(1)}, u32[]{:S(2)}, u32[]{:S(2)}) %collective-permute-start.33) | collective-permute-done | bytes 69664 | tf_op jit(solution)/shard_map/ppermute | solution.py:587
  19.2 0.9 stack.2
  20.1 1.5 %collective-permute-start.34 = (f32[56,128]{1,0:T(8,128)S(1)}, f32[56,128]{1,0:T(8,128)S(1)}, u32[]{:S(2)}, u32[]{:S(2)}) collective-permute-start(f32[56,128]{1,0:T(8,128)S(1)} %get-tuple-element.108), channel_id=1, source_target_pairs={{0,16},{16,0},{32,48},{48,32},{64,80},{80,64},{96,112},{112,96},{1... | collective-permute-start | bytes 86024 | tf_op jit(solution)/shard_map/ppermute | solution.py:587
  21.6 6.7 %collective-permute-start.35 = (f32[56,128]{1,0:T(8,128)S(1)}, f32[56,128]{1,0:T(8,128)S(1)}, u32[]{:S(2)}, u32[]{:S(2)}) collective-permute-start(f32[56,128]{1,0:T(8,128)S(1)} %get-tuple-element.109), channel_id=1, source_target_pairs={{16,32},{32,16},{48,64},{64,48},{80,96},{96,80},{112,128},{128,112... | collective-permute-start | bytes 86024 | tf_op jit(solution)/shard_map/ppermute | solution.py:587
  28.3 0.0 collective-permute-done.34.one_ref
  28.3 1.3 %collective-permute-done.35.two_ref = f32[56,128]{1,0:T(8,128)S(1)} collective-permute-done((f32[56,128]{1,0:T(8,128)S(1)}, f32[56,128]{1,0:T(8,128)S(1)}, u32[]{:S(2)}, u32[]{:S(2)}) %collective-permute-start.35) | collective-permute-done | bytes 28704 | tf_op jit(solution)/shard_map/ppermute | solution.py:587
  29.6 0.0 copy-done.5
  29.6 0.8 ghosts.2
  30.4 1.6 %collective-permute-start.36 = (f32[56,128]{1,0:T(8,128)S(1)}, f32[56,128]{1,0:T(8,128)S(1)}, u32[]{:S(2)}, u32[]{:S(2)}) collective-permute-start(f32[56,128]{1,0:T(8,128)S(1)} %get-tuple-element.114.sent_one), channel_id=1, source_target_pairs={{0,1},{1,0},{2,3},{3,2},{4,5},{5,4},{6,7},{7,6},{8,9},{9,8},{10,11... | collective-permute-start | bytes 86024 | tf_op jit(solution)/shard_map/ppermute | solution.py:587
  32.0 0.9 collective-permute-start.37
  32.8 0.0 collective-permute-done.36.got_one
  32.8 2.5 %collective-permute-done.37.got_two = f32[56,128]{1,0:T(8,128)S(1)} collective-permute-done((f32[56,128]{1,0:T(8,128)S(1)}, f32[56,128]{1,0:T(8,128)S(1)}, u32[]{:S(2)}, u32[]{:S(2)}) %collective-permute-start.37) | collective-permute-done | bytes 28704 | tf_op jit(solution)/shard_map/ppermute | solution.py:587
  35.3 0.0 copy-done.1
  35.3 0.0 copy-done.3
  35.3 1.2 %collide.2 = (f32[38,4,16,128]{3,2,1,0:T(8,128)S(1)}, f32[20,16,128]{2,1,0:T(8,128)S(1)}, f32[11,8,128]{2,1,0:T(8,128)S(1)}, f32[224,128]{1,0:T(8,128)S(1)}, f32[224,128]{1,0:T(8,128)S(1)}) custom-call(f32[8,32,128]{2,1,0:T(8,128)S(1)} %get-tuple-element.113.phase_ref, f32[56,128]{1,0:T(8,128)S(1)} %get-tuple-element.114.sent_one, ...), custom_call_target="tpu_custom_call" | custom-call | tf_op jit(solution)/shard_map/collide/pallas_call | solution.py:69
  36.5 0.1 collective-permute-start.38
  36.6 6.1 %collective-permute-start.39 = (f32[224,128]{1,0:T(8,128)S(1)}, f32[224,128]{1,0:T(8,128)S(1)}, u32[]{:S(2)}, u32[]{:S(2)}) collective-permute-start(f32[224,128]{1,0:T(8,128)S(1)} %get-tuple-element.120), channel_id=1, source_target_pairs={{16,32},{32,16},{48,64},{64,48},{80,96},{96,80},{112,128},{128,112... | collective-permute-start | bytes 344072 | tf_op jit(solution)/shard_map/ppermute | solution.py:587
  42.6 0.0 collective-permute-done.38.one_ref
  42.6 4.8 %collective-permute-done.39.two_ref = f32[224,128]{1,0:T(8,128)S(1)} collective-permute-done((f32[224,128]{1,0:T(8,128)S(1)}, f32[224,128]{1,0:T(8,128)S(1)}, u32[]{:S(2)}, u32[]{:S(2)}) %collective-permute-start.39) | collective-permute-done | bytes 114720 | tf_op jit(solution)/shard_map/ppermute | solution.py:587
  47.5 1.4 %stream.2 = (f32[19,4,16,128]{3,2,1,0:T(8,128)S(1)}, f32[19,4,16,128]{3,2,1,0:T(8,128)S(1)}, f32[4,16,128]{2,1,0:T(8,128)S(1)}, f32[17,4,128]{2,1,0:T(4,128)S(1)...) custom-call(s32[2,4]{1,0:T(2,128)S(1)} %copy-done.4, f32[4]{0:T(128)S(1)} %copy-done.5, ...), custom_call_target="tpu_custom_call" | custom-call | tf_op jit(solution)/shard_map/stream/pallas_call | solution.py:69
  48.9 1.1 %collective-permute-start.40 = (f32[17,4,128]{2,1,0:T(4,128)S(1)}, f32[17,4,128]{2,1,0:T(4,128)S(1)}, u32[]{:S(2)}, u32[]{:S(2)}) collective-permute-start(f32[17,4,128]{2,1,0:T(4,128)S(1)} %get-tuple-element.123), channel_id=1, source_target_pairs={{0,1},{1,0},{2,3},{3,2},{4,5},{5,4},{6,7},{7,6},{8,9},{9,8},{10,11... | collective-permute-start | bytes 104456 | tf_op jit(solution)/shard_map/ppermute | solution.py:587
  50.6 0.2 collective-permute-done.40.got_ref
  50.8 5.1 %conditional.3 = (f32[2,17,4,128]{3,2,1,0:T(4,128)}) conditional(s32[]{:T(128)} %bitcast.1, f32[2,17,4,128]{3,2,1,0:T(4,128)S(1)} %pair.3, f32[2,17,4,128]{3,2,1,0:T(4,128)S(1)} %pair.3, f32[2,17,4,128]{3,2,1,0:T(4,128)S(1)} %pair.3, f32[2,17,4,128]{3,2,1,0:T(4,128)S(1)} %pair.3, ...), branch_computations={%region_16.17_spmd, %region_17.18_spmd, %region_18.19_spmd, %regio... | conditional | bytes 278576 | solution.py:611
  50.8 3.0 %collective-permute-start.16 = (f32[2,17,4,128]{3,2,1,0:T(4,128)S(1)}, f32[2,17,4,128]{3,2,1,0:T(4,128)}, u32[]{:S(2)}, u32[]{:S(2)}) collective-permute-start(f32[2,17,4,128]{3,2,1,0:T(4,128)S(1)} %param.16), channel_id=1, source_target_pairs={{0,5},{5,0},{2,7},{7,2},{4,9},{9,4},{6,11},{11,6},{8,13},{13,8},{1... | collective-permute-start | bytes 208904 | tf_op jit(solution)/shard_map/cond/branch_0_fun/ppermute | solution.py:609
  53.8 2.1 %collective-permute-done.16 = f32[2,17,4,128]{3,2,1,0:T(4,128)} collective-permute-done((f32[2,17,4,128]{3,2,1,0:T(4,128)S(1)}, f32[2,17,4,128]{3,2,1,0:T(4,128)}, u32[]{:S(2)}, u32[]{:S(2)}) %collective-permute-start.16) | collective-permute-done | bytes 69664 | tf_op jit(solution)/shard_map/cond/branch_0_fun/ppermute | solution.py:609
  55.9 7.9 %collective-permute-start.41 = (f32[2,17,4,128]{3,2,1,0:T(4,128)}, f32[2,17,4,128]{3,2,1,0:T(4,128)S(1)}, u32[]{:S(2)}, u32[]{:S(2)}) collective-permute-start(f32[2,17,4,128]{3,2,1,0:T(4,128)} %get-tuple-element.143.crossed_ref), channel_id=1, source_target_pairs={{0,1},{1,0},{2,3},{3,2},{4,5},{5,4},{6,7},{7,6},{8,9},{9,8},{10,11... | collective-permute-start | bytes 208904 | tf_op jit(solution)/shard_map/ppermute | solution.py:587
  63.8 1.1 %collective-permute-done.41.other_ref = f32[2,17,4,128]{3,2,1,0:T(4,128)S(1)} collective-permute-done((f32[2,17,4,128]{3,2,1,0:T(4,128)}, f32[2,17,4,128]{3,2,1,0:T(4,128)S(1)}, u32[]{:S(2)}, u32[]{:S(2)}) %collective-permute-start.41) | collective-permute-done | bytes 69664 | tf_op jit(solution)/shard_map/ppermute | solution.py:587
  64.9 0.9 stack.3
  65.8 0.1 collective-permute-start.42
  65.9 1.9 %collective-permute-start.43 = (f32[56,128]{1,0:T(8,128)S(1)}, f32[56,128]{1,0:T(8,128)S(1)}, u32[]{:S(2)}, u32[]{:S(2)}) collective-permute-start(f32[56,128]{1,0:T(8,128)S(1)} %get-tuple-element.126), channel_id=1, source_target_pairs={{16,32},{32,16},{48,64},{64,48},{80,96},{96,80},{112,128},{128,112... | collective-permute-start | bytes 86024 | tf_op jit(solution)/shard_map/ppermute | solution.py:587
  67.8 0.8 collective-permute-done.42.one_ref
  68.6 4.6 %collective-permute-done.43.two_ref = f32[56,128]{1,0:T(8,128)S(1)} collective-permute-done((f32[56,128]{1,0:T(8,128)S(1)}, f32[56,128]{1,0:T(8,128)S(1)}, u32[]{:S(2)}, u32[]{:S(2)}) %collective-permute-start.43) | collective-permute-done | bytes 28704 | tf_op jit(solution)/shard_map/ppermute | solution.py:587
  73.3 0.8 ghosts.3
  74.1 1.3 %collective-permute-start.44 = (f32[56,128]{1,0:T(8,128)S(1)}, f32[56,128]{1,0:T(8,128)S(1)}, u32[]{:S(2)}, u32[]{:S(2)}) collective-permute-start(f32[56,128]{1,0:T(8,128)S(1)} %get-tuple-element.131.sent_one), channel_id=1, source_target_pairs={{0,1},{1,0},{2,3},{3,2},{4,5},{5,4},{6,7},{7,6},{8,9},{9,8},{10,11... | collective-permute-start | bytes 86024 | tf_op jit(solution)/shard_map/ppermute | solution.py:587
  75.3 0.3 collective-permute-start.45
  75.7 0.5 collective-permute-done.44.got_one
  76.2 2.5 %collective-permute-done.45.got_two = f32[56,128]{1,0:T(8,128)S(1)} collective-permute-done((f32[56,128]{1,0:T(8,128)S(1)}, f32[56,128]{1,0:T(8,128)S(1)}, u32[]{:S(2)}, u32[]{:S(2)}) %collective-permute-start.45) | collective-permute-done | bytes 28704 | tf_op jit(solution)/shard_map/ppermute | solution.py:587
  78.7 1.2 %collide.3 = (f32[38,4,16,128]{3,2,1,0:T(8,128)S(1)}, f32[20,16,128]{2,1,0:T(8,128)S(1)}, f32[11,8,128]{2,1,0:T(8,128)S(1)}, f32[224,128]{1,0:T(8,128)S(1)}, f32[224,128]{1,0:T(8,128)S(1)}) custom-call(f32[8,32,128]{2,1,0:T(8,128)S(1)} %get-tuple-element.130.phase_ref, f32[56,128]{1,0:T(8,128)S(1)} %get-tuple-element.131.sent_one, ...), custom_call_target="tpu_custom_call" | custom-call | tf_op jit(solution)/shard_map/collide/pallas_call | solution.py:69
  79.8 0.1 collective-permute-start.46
  79.9 1.9 %collective-permute-start.47 = (f32[224,128]{1,0:T(8,128)S(1)}, f32[224,128]{1,0:T(8,128)S(1)}, u32[]{:S(2)}, u32[]{:S(2)}) collective-permute-start(f32[224,128]{1,0:T(8,128)S(1)} %get-tuple-element.139), channel_id=1, source_target_pairs={{16,32},{32,16},{48,64},{64,48},{80,96},{96,80},{112,128},{128,112... | collective-permute-start | bytes 344072 | tf_op jit(solution)/shard_map/ppermute | solution.py:587
  81.9 2.8 %collective-permute-done.46.one_ref = f32[224,128]{1,0:T(8,128)S(1)} collective-permute-done((f32[224,128]{1,0:T(8,128)S(1)}, f32[224,128]{1,0:T(8,128)S(1)}, u32[]{:S(2)}, u32[]{:S(2)}) %collective-permute-start.46) | collective-permute-done | bytes 114720 | tf_op jit(solution)/shard_map/ppermute | solution.py:587
  84.6 6.9 %collective-permute-done.47.two_ref = f32[224,128]{1,0:T(8,128)S(1)} collective-permute-done((f32[224,128]{1,0:T(8,128)S(1)}, f32[224,128]{1,0:T(8,128)S(1)}, u32[]{:S(2)}, u32[]{:S(2)}) %collective-permute-start.47) | collective-permute-done | bytes 114720 | tf_op jit(solution)/shard_map/ppermute | solution.py:587
  91.6 2.1 %stream.3 = (f32[19,4,16,128]{3,2,1,0:T(8,128)}, f32[19,4,16,128]{3,2,1,0:T(8,128)}) custom-call(s32[2,4]{1,0:T(2,128)S(1)} %copy-done.4, f32[4]{0:T(128)S(1)} %copy-done.5, f32[38,4,16,128]{3,2,1,0:T(8,128)S(1)} %get-tuple-element.135.post_ref, f32[20,16,128]{2,1,0:T(8,128)S(1)} %get-tuple-element.136.columns_ref, ...), custom_call_target="tpu_custom_call" | custom-call | tf_op jit(solution)/shard_map/stream/pallas_call | solution.py:69
  (3 shorter events, 0.0 us)
Async XLA Ops:
  0.6 1.1 %copy-start = (f32[19,4,16,128]{3,2,1,0:T(8,128)S(1)}, f32[19,4,16,128]{3,2,1,0:T(8,128)}, u32[]{:S(2)}) copy-start(f32[19,4,16,128]{3,2,1,0:T(8,128)} %f_ref.3) | copy-start | bytes 1867780
  1.7 1.1 %copy-start.2 = (f32[19,4,16,128]{3,2,1,0:T(8,128)S(1)}, f32[19,4,16,128]{3,2,1,0:T(8,128)}, u32[]{:S(2)}) copy-start(f32[19,4,16,128]{3,2,1,0:T(8,128)} %g_ref.3) | copy-start | bytes 1867780
  2.8 3.6 %copy-start.4 = (s32[2,4]{1,0:T(2,128)S(1)}, s32[2,4]{1,0:T(2,128)}, u32[]{:S(2)}) copy-start(s32[2,4]{1,0:T(2,128)} %offsets.7) | copy-start | bytes 100
  2.8 26.8 %copy-start.5 = (f32[4]{0:T(128)S(1)}, f32[4]{0:T(128)}, u32[]{:S(2)}) copy-start(f32[4]{0:T(128)} %weights.7) | copy-start | bytes 52
  2.8 32.5 %copy-start.1 = (f32[19,4,16,128]{3,2,1,0:T(8,128)S(1)}, f32[19,4,16,128]{3,2,1,0:T(8,128)}, u32[]{:S(2)}) copy-start(f32[19,4,16,128]{3,2,1,0:T(8,128)} %f_ref.3) | copy-start | bytes 1867780
  2.8 32.5 %copy-start.3 = (f32[19,4,16,128]{3,2,1,0:T(8,128)S(1)}, f32[19,4,16,128]{3,2,1,0:T(8,128)}, u32[]{:S(2)}) copy-start(f32[19,4,16,128]{3,2,1,0:T(8,128)} %g_ref.3) | copy-start | bytes 1867780
  3.1 4.8 %collective-permute-start.32 = (f32[17,4,128]{2,1,0:T(4,128)S(1)}, f32[17,4,128]{2,1,0:T(4,128)S(1)}, u32[]{:S(2)}, u32[]{:S(2)}) collective-permute-start(f32[17,4,128]{2,1,0:T(4,128)S(1)} %get-tuple-element.106), channel_id=1, source_target_pairs={{0,1},{1,0},{2,3},{3,2},{4,5},{5,4},{6,7},{7,6},{8,9},{9,8},{10,11... | collective-permute-start | bytes 104456 | tf_op jit(solution)/shard_map/ppermute | solution.py:587
  7.9 9.8 %collective-permute-start.9 = (f32[2,17,4,128]{3,2,1,0:T(4,128)S(1)}, f32[2,17,4,128]{3,2,1,0:T(4,128)}, u32[]{:S(2)}, u32[]{:S(2)}) collective-permute-start(f32[2,17,4,128]{3,2,1,0:T(4,128)S(1)} %param.9), channel_id=1, source_target_pairs={{0,149},{149,0},{2,151},{151,2},{4,153},{153,4},{6,155},{155,6},{8... | collective-permute-start | bytes 208904 | tf_op jit(solution)/shard_map/cond/branch_9_fun/ppermute | solution.py:609
  17.7 1.5 %collective-permute-start.33 = (f32[2,17,4,128]{3,2,1,0:T(4,128)}, f32[2,17,4,128]{3,2,1,0:T(4,128)S(1)}, u32[]{:S(2)}, u32[]{:S(2)}) collective-permute-start(f32[2,17,4,128]{3,2,1,0:T(4,128)} %get-tuple-element.142.crossed_ref), channel_id=1, source_target_pairs={{0,1},{1,0},{2,3},{3,2},{4,5},{5,4},{6,7},{7,6},{8,9},{9,8},{10,11... | collective-permute-start | bytes 208904 | tf_op jit(solution)/shard_map/ppermute | solution.py:587
  20.1 8.2 %collective-permute-start.34 = (f32[56,128]{1,0:T(8,128)S(1)}, f32[56,128]{1,0:T(8,128)S(1)}, u32[]{:S(2)}, u32[]{:S(2)}) collective-permute-start(f32[56,128]{1,0:T(8,128)S(1)} %get-tuple-element.108), channel_id=1, source_target_pairs={{0,16},{16,0},{32,48},{48,32},{64,80},{80,64},{96,112},{112,96},{1... | collective-permute-start | bytes 86024 | tf_op jit(solution)/shard_map/ppermute | solution.py:587
  21.6 8.0 %collective-permute-start.35 = (f32[56,128]{1,0:T(8,128)S(1)}, f32[56,128]{1,0:T(8,128)S(1)}, u32[]{:S(2)}, u32[]{:S(2)}) collective-permute-start(f32[56,128]{1,0:T(8,128)S(1)} %get-tuple-element.109), channel_id=1, source_target_pairs={{16,32},{32,16},{48,64},{64,48},{80,96},{96,80},{112,128},{128,112... | collective-permute-start | bytes 86024 | tf_op jit(solution)/shard_map/ppermute | solution.py:587
  30.4 2.4 %collective-permute-start.36 = (f32[56,128]{1,0:T(8,128)S(1)}, f32[56,128]{1,0:T(8,128)S(1)}, u32[]{:S(2)}, u32[]{:S(2)}) collective-permute-start(f32[56,128]{1,0:T(8,128)S(1)} %get-tuple-element.114.sent_one), channel_id=1, source_target_pairs={{0,1},{1,0},{2,3},{3,2},{4,5},{5,4},{6,7},{7,6},{8,9},{9,8},{10,11... | collective-permute-start | bytes 86024 | tf_op jit(solution)/shard_map/ppermute | solution.py:587
  32.0 3.3 %collective-permute-start.37 = (f32[56,128]{1,0:T(8,128)S(1)}, f32[56,128]{1,0:T(8,128)S(1)}, u32[]{:S(2)}, u32[]{:S(2)}) collective-permute-start(f32[56,128]{1,0:T(8,128)S(1)} %get-tuple-element.115.sent_two), channel_id=1, source_target_pairs={{1,2},{2,1},{3,0},{0,3},{5,6},{6,5},{7,4},{4,7},{9,10},{10,9},{11,... | collective-permute-start | bytes 86024 | tf_op jit(solution)/shard_map/ppermute | solution.py:587
  36.5 6.2 %collective-permute-start.38 = (f32[224,128]{1,0:T(8,128)S(1)}, f32[224,128]{1,0:T(8,128)S(1)}, u32[]{:S(2)}, u32[]{:S(2)}) collective-permute-start(f32[224,128]{1,0:T(8,128)S(1)} %get-tuple-element.119), channel_id=1, source_target_pairs={{0,16},{16,0},{32,48},{48,32},{64,80},{80,64},{96,112},{112,96},{1... | collective-permute-start | bytes 344072 | tf_op jit(solution)/shard_map/ppermute | solution.py:587
  36.6 10.9 %collective-permute-start.39 = (f32[224,128]{1,0:T(8,128)S(1)}, f32[224,128]{1,0:T(8,128)S(1)}, u32[]{:S(2)}, u32[]{:S(2)}) collective-permute-start(f32[224,128]{1,0:T(8,128)S(1)} %get-tuple-element.120), channel_id=1, source_target_pairs={{16,32},{32,16},{48,64},{64,48},{80,96},{96,80},{112,128},{128,112... | collective-permute-start | bytes 344072 | tf_op jit(solution)/shard_map/ppermute | solution.py:587
  48.9 1.9 %collective-permute-start.40 = (f32[17,4,128]{2,1,0:T(4,128)S(1)}, f32[17,4,128]{2,1,0:T(4,128)S(1)}, u32[]{:S(2)}, u32[]{:S(2)}) collective-permute-start(f32[17,4,128]{2,1,0:T(4,128)S(1)} %get-tuple-element.123), channel_id=1, source_target_pairs={{0,1},{1,0},{2,3},{3,2},{4,5},{5,4},{6,7},{7,6},{8,9},{9,8},{10,11... | collective-permute-start | bytes 104456 | tf_op jit(solution)/shard_map/ppermute | solution.py:587
  50.8 5.1 %collective-permute-start.16 = (f32[2,17,4,128]{3,2,1,0:T(4,128)S(1)}, f32[2,17,4,128]{3,2,1,0:T(4,128)}, u32[]{:S(2)}, u32[]{:S(2)}) collective-permute-start(f32[2,17,4,128]{3,2,1,0:T(4,128)S(1)} %param.16), channel_id=1, source_target_pairs={{0,5},{5,0},{2,7},{7,2},{4,9},{9,4},{6,11},{11,6},{8,13},{13,8},{1... | collective-permute-start | bytes 208904 | tf_op jit(solution)/shard_map/cond/branch_0_fun/ppermute | solution.py:609
  55.9 9.0 %collective-permute-start.41 = (f32[2,17,4,128]{3,2,1,0:T(4,128)}, f32[2,17,4,128]{3,2,1,0:T(4,128)S(1)}, u32[]{:S(2)}, u32[]{:S(2)}) collective-permute-start(f32[2,17,4,128]{3,2,1,0:T(4,128)} %get-tuple-element.143.crossed_ref), channel_id=1, source_target_pairs={{0,1},{1,0},{2,3},{3,2},{4,5},{5,4},{6,7},{7,6},{8,9},{9,8},{10,11... | collective-permute-start | bytes 208904 | tf_op jit(solution)/shard_map/ppermute | solution.py:587
  65.8 2.8 %collective-permute-start.42 = (f32[56,128]{1,0:T(8,128)S(1)}, f32[56,128]{1,0:T(8,128)S(1)}, u32[]{:S(2)}, u32[]{:S(2)}) collective-permute-start(f32[56,128]{1,0:T(8,128)S(1)} %get-tuple-element.125), channel_id=1, source_target_pairs={{0,16},{16,0},{32,48},{48,32},{64,80},{80,64},{96,112},{112,96},{1... | collective-permute-start | bytes 86024 | tf_op jit(solution)/shard_map/ppermute | solution.py:587
  65.9 7.3 %collective-permute-start.43 = (f32[56,128]{1,0:T(8,128)S(1)}, f32[56,128]{1,0:T(8,128)S(1)}, u32[]{:S(2)}, u32[]{:S(2)}) collective-permute-start(f32[56,128]{1,0:T(8,128)S(1)} %get-tuple-element.126), channel_id=1, source_target_pairs={{16,32},{32,16},{48,64},{64,48},{80,96},{96,80},{112,128},{128,112... | collective-permute-start | bytes 86024 | tf_op jit(solution)/shard_map/ppermute | solution.py:587
  74.1 2.1 %collective-permute-start.44 = (f32[56,128]{1,0:T(8,128)S(1)}, f32[56,128]{1,0:T(8,128)S(1)}, u32[]{:S(2)}, u32[]{:S(2)}) collective-permute-start(f32[56,128]{1,0:T(8,128)S(1)} %get-tuple-element.131.sent_one), channel_id=1, source_target_pairs={{0,1},{1,0},{2,3},{3,2},{4,5},{5,4},{6,7},{7,6},{8,9},{9,8},{10,11... | collective-permute-start | bytes 86024 | tf_op jit(solution)/shard_map/ppermute | solution.py:587
  75.3 3.3 %collective-permute-start.45 = (f32[56,128]{1,0:T(8,128)S(1)}, f32[56,128]{1,0:T(8,128)S(1)}, u32[]{:S(2)}, u32[]{:S(2)}) collective-permute-start(f32[56,128]{1,0:T(8,128)S(1)} %get-tuple-element.132.sent_two), channel_id=1, source_target_pairs={{1,2},{2,1},{3,0},{0,3},{5,6},{6,5},{7,4},{4,7},{9,10},{10,9},{11,... | collective-permute-start | bytes 86024 | tf_op jit(solution)/shard_map/ppermute | solution.py:587
  79.8 4.8 %collective-permute-start.46 = (f32[224,128]{1,0:T(8,128)S(1)}, f32[224,128]{1,0:T(8,128)S(1)}, u32[]{:S(2)}, u32[]{:S(2)}) collective-permute-start(f32[224,128]{1,0:T(8,128)S(1)} %get-tuple-element.138), channel_id=1, source_target_pairs={{0,16},{16,0},{32,48},{48,32},{64,80},{80,64},{96,112},{112,96},{1... | collective-permute-start | bytes 344072 | tf_op jit(solution)/shard_map/ppermute | solution.py:587
  79.9 11.6 %collective-permute-start.47 = (f32[224,128]{1,0:T(8,128)S(1)}, f32[224,128]{1,0:T(8,128)S(1)}, u32[]{:S(2)}, u32[]{:S(2)}) collective-permute-start(f32[224,128]{1,0:T(8,128)S(1)} %get-tuple-element.139), channel_id=1, source_target_pairs={{16,32},{32,16},{48,64},{64,48},{80,96},{96,80},{112,128},{128,112... | collective-permute-start | bytes 344072 | tf_op jit(solution)/shard_map/ppermute | solution.py:587
